TPU v7x, 256 devices: a whole 4x4x8 slice. The times are simulated.
256 devices in a mesh: row: 64 (over x, z, core), col: 4 (over y).
Axes of the slice: x: 4, y: 4, z: 8, core: 2. Of those that a mesh axis runs over, the one named last changes fastest.
Arguments:
- krylov: float32 [8, 1024, 256], P(None, 'row'), may hold values from -8 to 8
- self_weight: float32 [1024, 256], P('row'), may hold values from 0.5 to 2
- cluster_basis: bfloat16 [1024, 64, 256], P('row'), may hold values from -0.375 to 0.375
- transfer: float32 [1024, 64, 64], P('row'), may hold values from -0.75 to 0.75
- near_blocks: bfloat16 [1024, 8, 256, 256], P('row', 'col'), may hold values from -0.125 to 0.125
- near_cols: int32 [1024, 8], P('row', 'col'), may hold values from 0 to 1023, as said below
- far_row: int32 [64, 4, 64], P('row', 'col'), may hold values from 0 to 1023, as said below
- far_col: int32 [64, 4, 64], P('row', 'col'), may hold values from 0 to 1023, as said below
- far_mat: float32 [64, 4, 64, 64, 64], P('row', 'col'), may hold values from -0.1875 to 0.1875
- coarse_row: int32 [64, 4, 16], P('row', 'col'), may hold values from 0 to 255, as said below
- coarse_col: int32 [64, 4, 16], P('row', 'col'), may hold values from 0 to 255, as said below
- coarse_mat: float32 [64, 4, 16, 64, 64], P('row', 'col'), may hold values from -0.1875 to 0.1875
Outputs:
- new_vectors: float32 [2, 1024, 256], P(None, 'row')
- hessen: float32 [2, 10], replicated
Inputs may be any that keep to these rules, and one draw needn't show every extreme that they name: `near_cols`: each near-field column leaf lies within 16 leaves of its row leaf, counted cyclically over 1024; both ends of that reach occur. `far_row`: blocks at row index r have row leaves r * 16 to (r + 1) * 16 - 1. `far_col`: blocks in column group c have column leaves equal to c modulo 4. `coarse_row`: blocks at row index r have row parents r * 4 to (r + 1) * 4 - 1. `coarse_col`: blocks in column group c have column parents equal to c modulo 4.
All inputs are finite; a program needn't handle non-finite values.
Results may differ from a plain program's by a relative error of at most 0.0025.
Values may be sent and summed in bfloat16 or wider, within the bound.
A program may use at most 64 MiB of HBM per device.

v0:
```python
import jax
import jax.numpy as jnp
from jax import lax
from jax.sharding import PartitionSpec as P

CHILD = 4


HIGH = lax.Precision.HIGHEST


def extended(cells, sides, width):
    for axis, dim in sides:
        count = lax.axis_size(axis)
        head = lax.slice_in_dim(cells, 0, width, axis=dim)
        tail = lax.slice_in_dim(cells, cells.shape[dim] - width, cells.shape[dim], axis=dim)
        cells = jnp.concatenate(
            [
                lax.ppermute(tail, axis, [(i, (i + 1) % count) for i in range(count)]),
                cells,
                lax.ppermute(head, axis, [((i + 1) % count, i) for i in range(count)]),
            ],
            axis=dim,
        )
    return cells


def apply_operator(
    v,
    self_weight,
    cluster_basis,
    transfer,
    near_blocks,
    near_cols,
    far_row,
    far_col,
    far_mat,
    coarse_row,
    coarse_col,
    coarse_mat,
):
    leaf_dev = v.shape[0]
    rank_size = cluster_basis.shape[1]
    leaves = leaf_dev * lax.axis_size("row")
    par_dev = leaf_dev // CHILD
    start = lax.axis_index("row") * leaf_dev
    vb = v.astype(jnp.bfloat16)
    coef = jnp.einsum("jap,jp->ja", cluster_basis, vb, preferred_element_type=jnp.float32)
    lifted = jnp.einsum("kab,ka->kb", transfer, coef, precision=HIGH)
    pcoef = lifted.reshape(par_dev, CHILD, rank_size).sum(axis=1)
    padded = extended(vb, (("row", 0),), leaf_dev)
    local_index = (near_cols - start + leaf_dev + leaves) % leaves
    picked = padded[local_index]
    near = jnp.einsum("ispq,isq->ip", near_blocks, picked, preferred_element_type=jnp.float32)
    cols_flat = far_col.reshape(-1)
    table = lax.all_gather(coef, "row", axis=0, tiled=True)
    taken = table[cols_flat]
    contrib = jnp.einsum(
        "bac,bc->ba", far_mat.reshape(-1, rank_size, rank_size), taken, precision=HIGH
    )
    leaf_onehot = (
        far_row.reshape(-1)[None, :] - start == jnp.arange(leaf_dev, dtype=jnp.int32)[:, None]
    ).astype(jnp.float32)
    far = jnp.dot(leaf_onehot, contrib, precision=HIGH)
    ptable = lax.all_gather(pcoef, "row", axis=0, tiled=True)
    ccontrib = jnp.einsum(
        "bac,bc->ba",
        coarse_mat.reshape(-1, rank_size, rank_size),
        ptable[coarse_col.reshape(-1)],
        precision=HIGH,
    )
    parent_onehot = (
        coarse_row.reshape(-1)[None, :] - lax.axis_index("row") * par_dev
        == jnp.arange(par_dev, dtype=jnp.int32)[:, None]
    ).astype(jnp.float32)
    cres = jnp.dot(parent_onehot, ccontrib, precision=HIGH)
    down = jnp.einsum("kab,kb->ka", transfer, jnp.repeat(cres, CHILD, axis=0), precision=HIGH)
    near_total, far_total = lax.psum((near, far + down), "col")
    farb = far_total.astype(jnp.bfloat16)
    back = jnp.einsum("jap,ja->jp", cluster_basis, farb, preferred_element_type=jnp.float32)
    return self_weight * v + near_total + back


def shards(
    krylov,
    self_weight,
    cluster_basis,
    transfer,
    near_blocks,
    near_cols,
    far_row,
    far_col,
    far_mat,
    coarse_row,
    coarse_col,
    coarse_mat,
):
    leaf_dev = krylov.shape[1]
    panels = krylov.shape[2]
    count = float(leaf_dev * lax.axis_size("row") * panels)
    vectors = krylov
    current = krylov[krylov.shape[0] - 1]
    outputs = []
    columns = []
    for step in range(2):
        w = apply_operator(
            current,
            self_weight,
            cluster_basis,
            transfer,
            near_blocks,
            near_cols,
            far_row,
            far_col,
            far_mat,
            coarse_row,
            coarse_col,
            coarse_mat,
        )
        local_proj = jnp.einsum("kip,ip->k", vectors, w, precision=HIGH)
        proj = lax.psum(local_proj, "row") / count
        w2 = w - jnp.einsum("k,kip->ip", proj, vectors, precision=HIGH)
        beta = jnp.sqrt(lax.psum(jnp.sum(w2 * w2), "row") / count + 1e-06)
        current = w2 / beta
        outputs.append(current)
        vectors = jnp.concatenate([vectors, current[None]], axis=0)
        if step == 0:
            columns.append(jnp.concatenate([proj, jnp.zeros((1,), jnp.float32), beta[None]]))
        else:
            columns.append(jnp.concatenate([proj, beta[None]]))
    return (jnp.stack(outputs), jnp.stack(columns))


def solution(mesh):
    in_specs = (
        P(None, "row", None),
        P("row", None),
        P("row", None, None),
        P("row", None, None),
        P("row", "col", None, None),
        P("row", "col"),
        P("row", "col", None),
        P("row", "col", None),
        P("row", "col", None, None, None),
        P("row", "col", None),
        P("row", "col", None),
        P("row", "col", None, None, None),
    )
    out_specs = (P(None, "row", None), P())
    return jax.shard_map(shards, mesh=mesh, in_specs=in_specs, out_specs=out_specs, check_vma=False)
```

profile of v0, /device:TPU:1, one launch (start us, length us, event | category | flops | bytes accessed | tf_op | source)
XLA Modules:
  0.0 772.3 jit_solution(7713722623563554580)
XLA Ops:
  0.6 0.9 bitcast_convert_fusion
  1.5 3.2 collective-permute-start.1
  4.8 0.7 fusion.67
  5.5 0.7 compare_select_fusion
  6.3 1.3 fusion.19
  7.6 1.6 fusion.23
  9.2 54.7 %all-gather = f32[64,4,64]{2,1,0:T(4,128)S(1)} all-gather(f32[1,4,64]{2,1,0:T(4,128)S(1)} %bitcast.194), channel_id=1, replica_groups=mesh['row'=64,'col'=4] {'row'}, dimensions={0}, use_global_device_ids=true | all-gather | bytes 66560 | tf_op jit(solution)/shard_map/all_gather | solution.py:65
  64.0 0.7 fusion.37
  64.6 0.6 gather_fusion.2
  65.2 2.0 fusion.6
  67.2 0.7 subtract_bitcast_fusion
  68.0 2.0 fusion.42
  69.9 47.5 %all_gather.12 = f32[1024,64]{1,0:T(8,128)S(1)} all-gather(f32[16,64]{1,0:T(8,128)S(1)} %bitcast.178), channel_id=1, replica_groups=mesh['row'=64,'col'=4] {'row'}, dimensions={0}, use_global_device_ids=true | all-gather | bytes 266240 | tf_op jit(solution)/shard_map/all_gather | solution.py:56
  117.5 0.7 fusion.36
  118.1 0.7 subtract_bitcast_fusion.1
  118.8 0.6 gather_fusion.1
  119.4 3.4 fusion.2
  123.0 0.6 gather_fusion
  123.6 3.4 fusion.41
  127.0 13.5 %all-reduce.1 = (f32[16,256]{1,0:T(8,128)S(1)}, bf16[16,64]{1,0:T(8,128)(2,1)S(1)}) all-reduce(f32[16,256]{1,0:T(8,128)S(1)} %bitcast.176, f32[16,64]{1,0:T(8,128)S(1)} %convolution_add_fusion.1), channel_id=1, replica_groups=mesh['row'=64,'col'=4] {'col'}, use_global_device_ids=true, to_apply=%region_0.0 | all-reduce | flops 5120 | bytes 38912 | tf_op jit(solution)/shard_map/psum | solution.py:78
  140.5 1.2 fusion.27
  141.8 0.4 convolution_bitcast_fusion.1
  142.2 127.4 %psum.58 = f32[8]{0:T(128)S(1)} all-reduce(f32[8]{0:T(128)S(1)} %convolution_bitcast_fusion.1), channel_id=1, replica_groups=mesh['row'=64,'col'=4] {'row'}, use_global_device_ids=true, to_apply=%region_3.4 | all-reduce | flops 8 | bytes 64 | tf_op jit(solution)/shard_map/psum | solution.py:121
  269.5 0.3 fusion.11
  269.8 0.6 multiply_reduce_fusion.1
  270.4 124.7 %psum.59 = f32[]{:T(128)} all-reduce(f32[]{:T(128)} %multiply_reduce_fusion.1), channel_id=1, replica_groups=mesh['row'=64,'col'=4] {'row'}, use_global_device_ids=true, to_apply=%region_5.6 | all-reduce | flops 1 | bytes 8 | tf_op jit(solution)/shard_map/psum | solution.py:123
  395.8 0.7 collective-permute-start.3
  396.6 1.1 collective-permute-start.2
  397.7 1.3 fusion.16
  398.9 0.5 fusion.21
  399.5 48.2 %all-gather.1 = f32[64,4,64]{2,1,0:T(4,128)S(1)} all-gather(f32[1,4,64]{2,1,0:T(4,128)S(1)} %bitcast.193), channel_id=1, replica_groups=mesh['row'=64,'col'=4] {'row'}, dimensions={0}, use_global_device_ids=true | all-gather | bytes 66560 | tf_op jit(solution)/shard_map/all_gather | solution.py:65
  447.7 0.6 gather_fusion.5
  448.2 0.9 fusion.4
  449.3 0.9 fusion.44
  450.2 47.6 %all_gather.14 = f32[1024,64]{1,0:T(8,128)S(1)} all-gather(f32[16,64]{1,0:T(8,128)S(1)} %bitcast.179), channel_id=1, replica_groups=mesh['row'=64,'col'=4] {'row'}, dimensions={0}, use_global_device_ids=true | all-gather | bytes 266240 | tf_op jit(solution)/shard_map/all_gather | solution.py:56
  497.8 0.6 gather_fusion.4
  498.4 3.4 fusion
  502.0 0.6 gather_fusion.3
  502.6 3.4 fusion.43
  506.0 11.3 %all-reduce = (bf16[16,64]{1,0:T(8,128)(2,1)S(1)}, f32[16,256]{1,0:T(8,128)S(1)}) all-reduce(f32[16,64]{1,0:T(8,128)S(1)} %convolution_add_fusion, f32[16,256]{1,0:T(8,128)S(1)} %bitcast.177), channel_id=1, replica_groups=mesh['row'=64,'col'=4] {'col'}, use_global_device_ids=true, to_apply=%region_8.9 | all-reduce | flops 5120 | bytes 38912 | tf_op jit(solution)/shard_map/psum | solution.py:78
  517.3 0.2 fusion.25
  517.5 0.4 convolution_bitcast_fusion
  518.0 126.7 %psum.62 = f32[9]{0:T(128)S(1)} all-reduce(f32[9]{0:T(128)S(1)} %convolution_bitcast_fusion), channel_id=1, replica_groups=mesh['row'=64,'col'=4] {'row'}, use_global_device_ids=true, to_apply=%region_9.10 | all-reduce | flops 9 | bytes 72 | tf_op jit(solution)/shard_map/psum | solution.py:121
  644.7 0.3 fusion.8
  645.1 0.6 multiply_reduce_fusion
  645.7 124.7 %psum.63 = f32[]{:T(128)} all-reduce(f32[]{:T(128)} %multiply_reduce_fusion), channel_id=1, replica_groups=mesh['row'=64,'col'=4] {'row'}, use_global_device_ids=true, to_apply=%region_11.12 | all-reduce | flops 1 | bytes 8 | tf_op jit(solution)/shard_map/psum | solution.py:123
  771.1 0.6 pad_maximum_fusion.1
  771.7 0.6 pad_maximum_fusion.4
  (45 shorter events, 1.1 us)
Async XLA Ops:
  0.6 118.8 %copy-start = (f32[1,1,64,64,64]{4,3,2,1,0:T(8,128)S(1)}, f32[1,1,64,64,64]{4,3,2,1,0:T(8,128)}, u32[]{:S(2)}) copy-start(f32[1,1,64,64,64]{4,3,2,1,0:T(8,128)} %param.20) | copy-start | bytes 3145732
  1.5 121.4 %collective-permute-start.1 = (bf16[16,256]{1,0:T(8,128)(2,1)S(1)}, bf16[16,256]{1,0:T(8,128)(2,1)S(1)}, u32[]{:S(2)}, u32[]{:S(2)}) collective-permute-start(bf16[16,256]{1,0:T(8,128)(2,1)S(1)} %bitcast_convert_fusion), channel_id=1, source_target_pairs={{4,0},{8,4},{12,8},{16,12},{20,16},{24,20},{28,24},{32,28},{36,32}... | collective-permute-start | bytes 24584 | tf_op jit(solution)/shard_map/ppermute | solution.py:21
  4.8 118.2 %collective-permute-start = (bf16[16,256]{1,0:T(8,128)(2,1)S(1)}, bf16[16,256]{1,0:T(8,128)(2,1)S(1)}, u32[]{:S(2)}, u32[]{:S(2)}) collective-permute-start(bf16[16,256]{1,0:T(8,128)(2,1)S(1)} %bitcast_convert_fusion), channel_id=1, source_target_pairs={{0,4},{4,8},{8,12},{12,16},{16,20},{20,24},{24,28},{28,32},{32,36}... | collective-permute-start | bytes 24584 | tf_op jit(solution)/shard_map/ppermute | solution.py:19
  69.9 71.8 %copy-start.4 = (f32[8,16,256]{2,1,0:T(8,128)S(1)}, f32[8,16,256]{2,1,0:T(8,128)}, u32[]{:S(2)}) copy-start(f32[8,16,256]{2,1,0:T(8,128)} %param.12) | copy-start | bytes 393220
  69.9 71.8 %copy-start.5 = (f32[16,256]{1,0:T(8,128)S(1)}, f32[16,256]{1,0:T(8,128)}, u32[]{:S(2)}) copy-start(f32[16,256]{1,0:T(8,128)} %param.13) | copy-start | bytes 49156
  119.4 279.6 %copy-start.1 = (f32[16,64,64]{2,1,0:T(8,128)S(1)}, f32[16,64,64]{2,1,0:T(8,128)}, u32[]{:S(2)}) copy-start(f32[16,64,64]{2,1,0:T(8,128)} %param.15) | copy-start | bytes 786436
  119.4 328.8 %copy-start.2 = (f32[1,1,16,64,64]{4,3,2,1,0:T(8,128)S(1)}, f32[1,1,16,64,64]{4,3,2,1,0:T(8,128)}, u32[]{:S(2)}) copy-start(f32[1,1,16,64,64]{4,3,2,1,0:T(8,128)} %param.23) | copy-start | bytes 786436
  395.8 106.1 %collective-permute-start.3 = (bf16[16,256]{1,0:T(8,128)(2,1)S(1)}, bf16[16,256]{1,0:T(8,128)(2,1)S(1)}, u32[]{:S(2)}, u32[]{:S(2)}) collective-permute-start(bf16[16,256]{1,0:T(8,128)(2,1)S(1)} %get-tuple-element.6), channel_id=1, source_target_pairs={{4,0},{8,4},{12,8},{16,12},{20,16},{24,20},{28,24},{32,28},{36,32}... | collective-permute-start | bytes 24584 | tf_op jit(solution)/shard_map/ppermute | solution.py:21
  396.6 105.4 %collective-permute-start.2 = (bf16[16,256]{1,0:T(8,128)(2,1)S(1)}, bf16[16,256]{1,0:T(8,128)(2,1)S(1)}, u32[]{:S(2)}, u32[]{:S(2)}) collective-permute-start(bf16[16,256]{1,0:T(8,128)(2,1)S(1)} %get-tuple-element.6), channel_id=1, source_target_pairs={{0,4},{4,8},{8,12},{12,16},{16,20},{20,24},{24,28},{28,32},{32,36}... | collective-permute-start | bytes 24584 | tf_op jit(solution)/shard_map/ppermute | solution.py:19
  449.3 68.0 %copy-start.3 = (bf16[16,64,256]{2,1,0:T(8,128)(2,1)S(1)}, bf16[16,64,256]{2,1,0:T(8,128)(2,1)}, u32[]{:S(2)}) copy-start(bf16[16,64,256]{2,1,0:T(8,128)(2,1)} %param.14) | copy-start | bytes 1572868
where the time goes:
time: 773 us; the launch traced here: 772 us
  blocking collectives  726 us (94%)
  matrix products  27.3 us (4%)
    psum x2, blocking collectives, shards(): proj = lax.psum(local_proj, 'row') / count  254 us
    psum x2, blocking collectives, shards(): beta = jnp.sqrt(lax.psum(jnp.sum(w2 * w2), 'row') / count + 1e-06)  249 us
    all_gather x2, blocking collectives, apply_operator(): ptable = lax.all_gather(pcoef, 'row', axis=0, tiled=True)  103 us
    all_gather x2, blocking collectives, apply_operator(): table = lax.all_gather(coef, 'row', axis=0, tiled=True)  95.1 us
    psum x2, blocking collectives, apply_operator(): near_total, far_total = lax.psum((near, far + down), 'col')  24.8 us
  transfers between devices with their start and end apart: 4, of which 0 were waited for; matrix products, arithmetic and copies ran while one was open for 3% of the time, Pallas kernels for 0%

commit v1 on v0

v1 whole, which is shorter than its diff:
```python
import functools

import jax
import jax.numpy as jnp
from jax import lax
from jax.experimental import pallas as pl
from jax.experimental.pallas import tpu as pltpu
from jax.sharding import PartitionSpec as P

MESH = pl.DeviceIdType.MESH
F32 = jnp.float32
BF16 = jnp.bfloat16

NX, NZ, NCORE, NCOL = 4, 8, 2, 4
NROW = NX * NZ * NCORE
LEAF, PANEL, RANK, KRY = 16, 256, 64, 8
LEAVES = NROW * LEAF
FAR, COARSE = 64, 16
COUNT = float(LEAVES * PANEL)


def iota(shape, dim):
    return lax.broadcasted_iota(jnp.int32, shape, dim)


def nt(a, b):
    return lax.dot_general(a, b, (((1,), (1,)), ((), ())), preferred_element_type=F32)


def split(x):
    hi = x.astype(BF16)
    return hi, (x - hi.astype(F32)).astype(BF16)


def fold(x):
    s = x[:, :128] + x[:, 128:]
    return s + pltpu.roll(s, 64, 1)


def partial_sum(x):
    s = x[:8] + x[8:]
    return jnp.sum(s[:, :128] + s[:, 128:], axis=0, keepdims=True)


def lanes_of(rows, first):
    sums = jnp.sum(rows, axis=1, keepdims=True)
    n = rows.shape[0]
    return jnp.sum(jnp.where(iota((n, 128), 1) == iota((n, 128), 0) + first, sums, 0.0), axis=0, keepdims=True)


def stack_rows(rows, n):
    out = jnp.zeros((n, 128), F32)
    at = iota((n, 128), 0)
    for j, r in enumerate(rows):
        out = jnp.where(at == j, r, out)
    return out


def kernel(
    kry_h, sw_h, cb_h, tr_h, nb_h, fm_h, cm_h, nc_h, fr_h, fc_h, cr_h, cc_h,
    out_v, out_h,
    nc_s, fr_s, fc_s, cr_s, cc_s,
    kry, sw, cb, bfar, tr, nb, fm, cm,
    pb, ftile, ttile, fmask, fpar, gram_rows,
    pay, tab, halo_src, halo, vpad, grow, near_src, near_tab, far_src, far_tab, sc_src, sc_tab,
    load_sem, pay_s, pay_r, halo_s, halo_r, near_s, near_r, far_s, far_r, sc_s, sc_r,
):
    me = lax.axis_index("row")
    col = lax.axis_index("col")
    x = me // (NZ * NCORE)
    z = lax.rem(me // NCORE, NZ)
    core = lax.rem(me, NCORE)
    start = me * LEAF

    loads = []

    def load(src, dst):
        c = pltpu.make_async_copy(src, dst, load_sem.at[len(loads)])
        c.start()
        loads.append(c)
        return c

    l_kry = load(kry_h, kry)
    l_cb = load(cb_h, cb)
    l_bf = [load(cb_h.at[4 * k + col], bfar.at[k]) for k in range(4)]
    l_tr = load(tr_h, tr)
    l_fm = load(fm_h, fm)
    l_cm = load(cm_h, cm)
    l_nb = load(nb_h, nb)
    l_sw = load(sw_h, sw)
    l_index = [load(h, s) for h, s in ((nc_h, nc_s), (fr_h, fr_s), (fc_h, fc_s), (cr_h, cr_s), (cc_h, cc_s))]

    bar = pltpu.get_barrier_semaphore()

    def far_peer(k):
        jz = k // (NX * NCORE)
        rest = lax.rem(k, NX * NCORE)
        jx = rest // NCORE
        jc = lax.rem(rest, NCORE)
        dz = NZ // 2 + (1 - 2 * lax.rem(jz, 2)) * ((jz + 1) // 2) + NZ
        dx = NX // 2 + (1 - 2 * lax.rem(jx, 2)) * ((jx + 1) // 2) + NX
        pz = lax.rem(z + dz, NZ)
        px = lax.rem(x + dx, NX)
        pc = lax.rem(core + 1 + jc, NCORE)
        return (px * NZ + pz) * NCORE + pc

    def to_row(body):
        def step(k, c):
            body(far_peer(k))
            return c
        lax.fori_loop(0, NROW - 1, step, 0, unroll=7)

    to_row(lambda p: pl.semaphore_signal(bar, inc=1, device_id=(p, col), device_id_type=MESH))
    for k in range(1, NCOL):
        pl.semaphore_signal(bar, inc=1, device_id=(me, lax.rem(col + k, NCOL)), device_id_type=MESH)

    def remote(src, dst, ssem, rsem, dev):
        pltpu.make_async_remote_copy(
            src_ref=src, dst_ref=dst, send_sem=ssem, recv_sem=rsem, device_id=dev, device_id_type=MESH
        ).start()

    def wait(ref, sem):
        pltpu.make_async_copy(ref, ref, sem).wait()

    lane256 = iota((LEAF, PANEL), 1) // RANK
    row256 = iota((LEAF, PANEL), 0)

    l_kry.wait()
    l_cb.wait()
    l_tr.wait()
    for k in range(4):
        child = 4 * col + k
        prod = lax.dot_general(
            tr[child], cb[child].astype(F32), (((0,), (0,)), ((), ())),
            precision=lax.Precision.HIGHEST, preferred_element_type=F32,
        )
        hi, lo = split(prod)
        pb[0, RANK * k : RANK * (k + 1), :] = hi
        pb[1, RANK * k : RANK * (k + 1), :] = lo
    for c in l_bf:
        c.wait()

    far_pick = (row256 == 4 * lane256 + col).astype(F32)
    par_pick = (row256 == 4 * col + lane256).astype(F32)

    def coefficients(vb):
        a = nt(vb, bfar[...].reshape(4 * RANK, PANEL))
        b = nt(vb, pb[0]) + nt(vb, pb[1])
        a = jnp.sum(a * far_pick, axis=0, keepdims=True)
        b = jnp.sum(b * par_pick, axis=0, keepdims=True)
        return a[:, :128], a[:, 128:], fold(b)

    def set_pay(step, v, extra):
        vb = v.astype(BF16)
        c0, c1, p = coefficients(vb)
        pay[step, 0:1, :] = c0
        pay[step, 1:2, :] = c1
        low = iota((1, 128), 1) < RANK
        pay[step, 2:3, :] = jnp.where(low, p, extra) if extra is not None else p
        halo_src[step] = vb
        vpad[step, LEAF : 2 * LEAF, :] = vb.astype(F32)

    for k in range(KRY):
        for l in range(k, KRY):
            r = partial_sum(kry[k] * kry[l])
            gram_rows[8 * k + l : 8 * k + l + 1, :] = r
            if l > k:
                gram_rows[8 * l + k : 8 * l + k + 1, :] = r
    set_pay(0, kry[KRY - 1], lanes_of(gram_rows[...], 64))

    pl.semaphore_wait(bar, NROW - 1 + NCOL - 1)

    def send_pay(step):
        tab[step, me] = pay[step]
        to_row(lambda p: remote(pay.at[step], tab.at[step, me], pay_s.at[step], pay_r.at[step], (p, col)))
        up = lax.rem(me + 1, NROW)
        down = lax.rem(me + NROW - 1, NROW)
        remote(halo_src.at[step], halo.at[step, 0], halo_s.at[step, 0], halo_r.at[step, 0], (up, col))
        remote(halo_src.at[step], halo.at[step, 1], halo_s.at[step, 1], halo_r.at[step, 1], (down, col))

    send_pay(0)

    l_fm.wait()
    l_cm.wait()
    for c in l_index:
        c.wait()
    for t in range(5):
        for n in range(4):
            if t < 4:
                four = [fm[16 * t + 4 * n + k] for k in range(4)]
            else:
                four = [cm[4 * n + k] for k in range(4)]
            hi, lo = split(jnp.concatenate(four, axis=1))
            ftile[t, 0, RANK * n : RANK * (n + 1), :] = hi
            ftile[t, 1, RANK * n : RANK * (n + 1), :] = lo
    for j in range(4):
        hi, lo = split(jnp.concatenate([tr[4 * g + j] for g in range(4)], axis=1))
        ttile[0, RANK * j : RANK * (j + 1), :] = hi
        ttile[1, RANK * j : RANK * (j + 1), :] = lo

    for t in range(5):
        for n in range(4):
            row = jnp.zeros((LEAF, PANEL), jnp.int32)
            for k in range(4):
                if t < 4:
                    at = fr_s[16 * t + 4 * n + k] - start
                else:
                    at = cr_s[4 * n + k] - 4 * me
                row = jnp.where(lane256 == k, at, row)
            mine = row256 if t < 4 else row256 // 4
            fmask[t, LEAF * n : LEAF * (n + 1), :] = (row == mine).astype(F32)
    for b in range(FAR):
        half = lax.rem(fc_s[b] // 4, 2)
        fpar[b % 2, b // 2 : b // 2 + 1, :] = jnp.full((1, 128), half, jnp.int32)
    for b in range(COARSE):
        fpar[b % 2, 32 + b // 2 : 33 + b // 2, :] = jnp.zeros((1, 128), jnp.int32)

    diag = (iota((RANK, PANEL), 0) // LEAF == iota((RANK, PANEL), 1) // RANK).astype(F32)

    def near_part(step):
        wait(halo.at[step, 0], halo_r.at[step, 0])
        wait(halo.at[step, 1], halo_r.at[step, 1])
        vpad[step, 0:LEAF, :] = halo[step, 0].astype(F32)
        vpad[step, 2 * LEAF :, :] = halo[step, 1].astype(F32)

        def body(i, acc):
            out = jnp.zeros((LEAF, PANEL), F32)
            for s in range(2):
                at = jnp.minimum(lax.rem(nc_s[s, i] - start + LEAF + LEAVES, LEAVES), 3 * LEAF - 1)
                lhs = jnp.broadcast_to(vpad[step, pl.ds(at, 1), :], (LEAF, PANEL)).astype(BF16)
                out = out + nt(lhs, nb[i, s])
            return jnp.where(row256 == i, out, acc)

        near_src[step] = lax.fori_loop(0, LEAF, body, jnp.zeros((LEAF, PANEL), F32), unroll=4)
        near_tab[step, col] = near_src[step]
        for k in range(1, NCOL):
            remote(near_src.at[step], near_tab.at[step, col], near_s.at[step], near_r.at[step], (me, lax.rem(col + k, NCOL)))

    def product(t, rows, first):
        xs = []
        for n in range(4):
            r = jnp.concatenate([rows[first + 2 * n : first + 2 * n + 1], rows[first + 2 * n + 1 : first + 2 * n + 2]], axis=1)
            xs.append(jnp.broadcast_to(r, (LEAF, PANEL)))
        hi, lo = split(jnp.concatenate(xs, axis=0) * fmask[t])
        o = nt(jnp.concatenate([hi, lo], axis=0), ftile[t, 0])
        return o[:RANK] + o[RANK:] + nt(hi, ftile[t, 1])

    def over_groups(o):
        o = o * diag
        return (o[0:16] + o[16:32]) + (o[32:48] + o[48:64])

    def far_part(step):
        wait(tab.at[step, pl.ds(0, NROW - 1)], pay_r.at[step])
        for b in range(FAR):
            c = fc_s[b]
            grow[b % 2, b // 2 : b // 2 + 1, :] = tab[step, c // LEAF, pl.ds(lax.rem(c, LEAF) // 8, 1), :]
        for b in range(COARSE):
            grow[b % 2, 32 + b // 2 : 33 + b // 2, :] = tab[step, cc_s[b] // 4, 2:3, :]
        low = iota((40, 128), 1) < RANK
        even, odd = grow[0], grow[1]
        rows = jnp.where(
            low,
            jnp.where(fpar[0] == 0, even, pltpu.roll(even, 64, 1)),
            jnp.where(fpar[1] == 1, odd, pltpu.roll(odd, 64, 1)),
        )
        cres = fold(over_groups(product(4, rows, 32)))
        far = product(0, rows, 0) + product(1, rows, 8) + product(2, rows, 16) + product(3, rows, 24)
        hi, lo = split(jnp.concatenate([cres, cres], axis=1) * (lane256 == row256 // 4).astype(F32))
        o = nt(jnp.concatenate([hi, lo], axis=0), ttile[0])
        down = o[:LEAF] + o[LEAF:] + nt(hi, ttile[1])
        total = fold(over_groups(far) + down * (lane256 == lax.rem(row256, 4)).astype(F32))
        far_src[step] = jnp.where(iota((8, 128), 1) < RANK, total[:8], total[8:])
        far_tab[step, col] = far_src[step]
        for k in range(1, NCOL):
            remote(far_src.at[step], far_tab.at[step, col], far_s.at[step], far_r.at[step], (me, lax.rem(col + k, NCOL)))

    def assemble(step, v):
        wait(near_tab.at[step, pl.ds(0, NCOL - 1)], near_r.at[step])
        near = (near_tab[step, 0] + near_tab[step, 1]) + (near_tab[step, 2] + near_tab[step, 3])
        base = sw[...] * v + near
        wait(far_tab.at[step, pl.ds(0, NCOL - 1)], far_r.at[step])
        far = (far_tab[step, 0] + far_tab[step, 1]) + (far_tab[step, 2] + far_tab[step, 3])
        back = pltpu.roll(far, 64, 1)
        low = iota((8, 128), 1) < RANK
        both = jnp.concatenate([jnp.where(low, far, back), jnp.where(low, back, far)], axis=0)
        both = jnp.concatenate([both, both], axis=1).astype(BF16).astype(F32)
        for g in range(4):
            lhs = jnp.where(row256 == 4 * g + lane256, both, 0.0).astype(BF16)
            base = base + jnp.dot(lhs, cb[4 * g : 4 * g + 4].reshape(4 * RANK, PANEL), preferred_element_type=F32)
        return base

    def exchange(step, row):
        sc_src[step] = row
        sc_tab[step, me] = row
        to_row(lambda p: remote(sc_src.at[step], sc_tab.at[step, me], sc_s.at[step], sc_r.at[step], (p, col)))

    def exchanged(step):
        wait(sc_tab.at[step, pl.ds(0, NROW - 1)], sc_r.at[step])
        return jnp.sum(sc_tab[step], axis=0) * (1.0 / COUNT)

    lane1 = iota((1, 128), 1)
    sq = (iota((8, 128), 0) == iota((8, 128), 1))

    def pick(row, k):
        return row[:, k : k + 1]

    l_nb.wait()
    near_part(0)
    far_part(0)
    gsum = jnp.sum(tab[0], axis=0)[2:3] * (1.0 / COUNT)
    gram = jnp.zeros((8, 128), F32)
    for k in range(KRY):
        gram = jnp.where(iota((8, 128), 0) == k, pltpu.roll(gsum, 64 - 8 * k, 1), gram)
    gram = jnp.where(iota((8, 128), 1) < KRY, gram, 0.0)
    l_sw.wait()
    w = assemble(0, kry[KRY - 1])
    sums = [partial_sum(kry[k] * w) for k in range(KRY)] + [partial_sum(w * w)]
    exchange(0, lanes_of(stack_rows(sums, 16), 0))
    tot = exchanged(0)

    def quadratic(tot):
        gh = jnp.sum(gram * tot, axis=1, keepdims=True)
        hcol = jnp.sum(jnp.where(sq, tot, 0.0), axis=1, keepdims=True)
        return jnp.sum(gh * hcol, axis=0, keepdims=True)

    h_row = jnp.where(lane1 < KRY, tot, 0.0)
    hh = jnp.sum(h_row * h_row, axis=1, keepdims=True)
    norm = pick(tot, KRY) - 2.0 * hh + quadratic(h_row)
    beta = jnp.sqrt(jnp.maximum(norm, 0.0) + 1e-06)
    w2 = w
    for k in range(KRY):
        w2 = w2 - pick(tot, k) * kry[k]
    q = w2 / beta
    out_v[0] = q
    line = jnp.where(lane1 == KRY + 1, beta, h_row)
    out_h[0:1, :] = line[:, : KRY + 2]

    set_pay(1, q, None)
    send_pay(1)
    new_gram = [partial_sum(kry[k] * q) for k in range(KRY)] + [partial_sum(q * q)]
    near_part(1)
    far_part(1)
    w = assemble(1, q)
    sums = [partial_sum(kry[k] * w) for k in range(KRY)] + [partial_sum(q * w), partial_sum(w * w)]
    exchange(1, lanes_of(stack_rows(sums + [jnp.zeros((1, 128), F32)] * 6 + new_gram, 32), 0))
    tot = exchanged(1)
    h_all = jnp.where(lane1 <= KRY, tot, 0.0)
    h_row = jnp.where(lane1 < KRY, tot, 0.0)
    g_row = jnp.where(lane1 <= KRY, pltpu.roll(tot, 128 - 16, 1), 0.0)
    hh = jnp.sum(h_all * h_all, axis=1, keepdims=True)
    hg = jnp.sum(h_all * g_row, axis=1, keepdims=True)
    h8 = pick(tot, KRY)
    norm = pick(tot, KRY + 1) - 2.0 * hh + quadratic(h_row) + 2.0 * h8 * hg - h8 * h8 * pick(g_row, KRY)
    beta = jnp.sqrt(jnp.maximum(norm, 0.0) + 1e-06)
    w2 = w - h8 * q
    for k in range(KRY):
        w2 = w2 - pick(tot, k) * kry[k]
    out_v[1] = w2 / beta
    line = jnp.where(lane1 == KRY + 1, beta, h_all)
    out_h[1:2, :] = line[:, : KRY + 2]

    for step in range(2):
        wait(tab.at[step, pl.ds(0, NROW - 1)], pay_s.at[step])
        wait(halo.at[step, 0], halo_s.at[step, 0])
        wait(halo.at[step, 1], halo_s.at[step, 1])
        wait(near_tab.at[step, pl.ds(0, NCOL - 1)], near_s.at[step])
        wait(far_tab.at[step, pl.ds(0, NCOL - 1)], far_s.at[step])
        wait(sc_tab.at[step, pl.ds(0, NROW - 1)], sc_s.at[step])


def shards(krylov, self_weight, cluster_basis, transfer, near_blocks, near_cols, far_row, far_col, far_mat, coarse_row, coarse_col, coarse_mat):
    anywhere = pl.BlockSpec(memory_space=pl.ANY)
    S = pltpu.SMEM
    vmem = pl.BlockSpec(memory_space=pltpu.VMEM)
    V = pltpu.VMEM
    DMA = pltpu.SemaphoreType.DMA
    return pl.pallas_call(
        kernel,
        out_shape=(
            jax.ShapeDtypeStruct((2, LEAF, PANEL), F32),
            jax.ShapeDtypeStruct((2, KRY + 2), F32),
        ),
        in_specs=[anywhere] * 12,
        out_specs=(vmem, vmem),
        scratch_shapes=[
            S((2, LEAF), jnp.int32), S((FAR,), jnp.int32), S((FAR,), jnp.int32), S((COARSE,), jnp.int32), S((COARSE,), jnp.int32),
            V((KRY, LEAF, PANEL), F32),
            V((LEAF, PANEL), F32),
            V((LEAF, RANK, PANEL), BF16),
            V((4, RANK, PANEL), BF16),
            V((LEAF, RANK, RANK), F32),
            V((LEAF, 2, PANEL, PANEL), BF16),
            V((FAR, RANK, RANK), F32),
            V((COARSE, RANK, RANK), F32),
            V((2, 4 * RANK, PANEL), BF16),
            V((5, 2, 4 * RANK, 4 * RANK), BF16),
            V((2, 4 * RANK, 4 * RANK), BF16),
            V((5, 4 * LEAF, 4 * RANK), F32),
            V((2, 40, 128), jnp.int32),
            V((64, 128), F32),
            V((2, 3, 128), F32),
            V((2, NROW, 3, 128), F32),
            V((2, LEAF, PANEL), BF16),
            V((2, 2, LEAF, PANEL), BF16),
            V((2, 3 * LEAF, PANEL), F32),
            V((2, 40, 128), F32),
            V((2, LEAF, PANEL), F32),
            V((2, NCOL, LEAF, PANEL), F32),
            V((2, 8, 128), F32),
            V((2, NCOL, 8, 128), F32),
            V((2, 1, 128), F32),
            V((2, NROW, 1, 128), F32),
            DMA((16,)),
            DMA((2,)), DMA((2,)),
            DMA((2, 2)), DMA((2, 2)),
            DMA((2,)), DMA((2,)),
            DMA((2,)), DMA((2,)),
            DMA((2,)), DMA((2,)),
        ],
        compiler_params=pltpu.CompilerParams(
            collective_id=0, has_side_effects=True, vmem_limit_bytes=60 * 2**20
        ),
        name="hmatrix_gmres",
    )(
        krylov,
        self_weight,
        cluster_basis,
        transfer,
        near_blocks,
        far_mat.reshape(FAR, RANK, RANK),
        coarse_mat.reshape(COARSE, RANK, RANK),
        near_cols.T,
        far_row.reshape(FAR),
        far_col.reshape(FAR),
        coarse_row.reshape(COARSE),
        coarse_col.reshape(COARSE),
    )


def solution(mesh):
    in_specs = (
        P(None, "row", None),
        P("row", None),
        P("row", None, None),
        P("row", None, None),
        P("row", "col", None, None),
        P("row", "col"),
        P("row", "col", None),
        P("row", "col", None),
        P("row", "col", None, None, None),
        P("row", "col", None),
        P("row", "col", None),
        P("row", "col", None, None, None),
    )
    out_specs = (P(None, "row", None), P())
    return jax.shard_map(shards, mesh=mesh, in_specs=in_specs, out_specs=out_specs, check_vma=False)
```

time: 773 us -> 51.8 us (0.07)
  blocking collectives: 726 us -> 0 us
  Pallas kernels: 0 us -> 48.4 us
  matrix products: 27.3 us -> 0 us
    psum x6 -> x0, blocking collectives: 528 us -> none  [the longest x2 254 us: shards(): proj = lax.psum(local_proj, 'row') / count]
    all_gather x4 -> x0, blocking collectives: 198 us -> none  [the longest x2 103 us: apply_operator(): ptable = lax.all_gather(pcoef, 'row', axis=0, tiled=True)]
    pallas_call x0 -> x1, Pallas kernels: none -> 48.4 us  [shards(): pl.pallas_call(kernel, out_shape=(jax.ShapeDtypeStruct((2, LEAF, PANEL),...]
    dot_general x22 -> x0, matrix products: 27.3 us -> none  [the longest x2 6.73 us: apply_operator(): jnp.einsum('ispq,isq->ip', near_blocks, picked, preferred_element_type=jn...]
  transfers between devices with their start and end apart: 4 -> 0, of which waited for: 0 -> 0; matrix products, arithmetic and copies ran while one was open for 3% -> 0% of each run, Pallas kernels for 0% -> 0%
where the time goes in v1:
time: 51.8 us; the launch traced here: 51.7 us
  Pallas kernels  48.4 us (93%)
  local copies, waits for them, and re-layouts  2.6 us (5%)
  between operations  0.64 us (1%)
    pallas_call x1, Pallas kernels, shards(): pl.pallas_call(kernel, out_shape=(jax.ShapeDtypeStruct((2, LEAF, PANEL),...  48.4 us
    unnamed x2, local copies, waits for them, and re-layouts  2.6 us

profile of v1, /device:TPU:1, one launch (start us, length us, event | category | flops | bytes accessed | tf_op | source)
XLA Modules:
  0.0 51.7 jit_solution(4401916711793137202)
XLA Ops:
  0.6 48.4 %hmatrix_gmres.1 = (f32[2,16,256]{2,1,0:T(8,128)}, f32[2,10]{1,0:T(2,128)}) custom-call(f32[8,16,256]{2,1,0:T(8,128)} %kry_h.1, f32[16,256]{1,0:T(8,128)} %sw_h.1, bf16[16,64,256]{2,1,0:T(8,128)(2,1)} %cb_h.1, f32[16,64,64]{2,1,0:T(8,128)} %tr_h.1, bf16[16,2,256,256]{3,2,1,0:T(8,128)(2,1)} %nb_h.1, f32[64,64,64]{2,1,0:T(8,128)} %bitcast.7, ...), custom_call_target="tpu_custom_call" | custom-call | tf_op jit(solution)/shard_map/hmatrix_gmres/pallas_call | solution.py:377
  49.1 1.4 %copy.16 = f32[2,16,256]{2,1,0:T(8,128)} copy(f32[2,16,256]{2,1,0:T(8,128)} %get-tuple-element.4) | data formatting | bytes 65536
  50.4 1.2 %copy.17 = f32[2,10]{1,0:T(2,128)} copy(f32[2,10]{1,0:T(2,128)} %get-tuple-element.5) | data formatting | bytes 160

commit v2 on v1

--- a/solution.py
+++ b/solution.py
@@ -16,6 +16,7 @@
 LEAF, PANEL, RANK, KRY = 16, 256, 64, 8
 LEAVES = NROW * LEAF
 FAR, COARSE = 64, 16
+QROWS = 20
 COUNT = float(LEAVES * PANEL)
 
 
@@ -62,9 +63,10 @@
     nc_s, fr_s, fc_s, cr_s, cc_s,
     kry, sw, cb, bfar, tr, nb, fm, cm,
     pb, ftile, ttile, fmask, fpar, gram_rows,
-    pay, tab, halo_src, halo, vpad, grow, near_src, near_tab, far_src, far_tab, sc_src, sc_tab,
-    load_sem, pay_s, pay_r, halo_s, halo_r, near_s, near_r, far_s, far_r, sc_s, sc_r,
+    pay, tab_a, tab_b, halo_src, halo, vq, vpad_a, vpad_b, nq, qpay, qtab, qgrow, qrows, grow, near_src, near_tab, far_src, far_tab, sc_src, sc_tab,
+    load_sem, pay_s, pay_r, halo_s, halo_r, near_s, near_r, far_s, far_r, sc_s, sc_r, q_s, q_r, qf_s, qf_r, vq_s, vq_r,
 ):
+    tab, vpad = (tab_a, tab_b), (vpad_a, vpad_b)
     me = lax.axis_index("row")
     col = lax.axis_index("col")
     x = me // (NZ * NCORE)
@@ -143,22 +145,23 @@
     far_pick = (row256 == 4 * lane256 + col).astype(F32)
     par_pick = (row256 == 4 * col + lane256).astype(F32)
 
-    def coefficients(vb):
-        a = nt(vb, bfar[...].reshape(4 * RANK, PANEL))
-        b = nt(vb, pb[0]) + nt(vb, pb[1])
-        a = jnp.sum(a * far_pick, axis=0, keepdims=True)
-        b = jnp.sum(b * par_pick, axis=0, keepdims=True)
-        return a[:, :128], a[:, 128:], fold(b)
-
-    def set_pay(step, v, extra):
-        vb = v.astype(BF16)
-        c0, c1, p = coefficients(vb)
-        pay[step, 0:1, :] = c0
-        pay[step, 1:2, :] = c1
-        low = iota((1, 128), 1) < RANK
-        pay[step, 2:3, :] = jnp.where(low, p, extra) if extra is not None else p
-        halo_src[step] = vb
-        vpad[step, LEAF : 2 * LEAF, :] = vb.astype(F32)
+    def coefficients(hi, lo):
+        n = hi.shape[0] // LEAF
+        far = bfar[...].reshape(4 * RANK, PANEL)
+        a, b = nt(hi, far), nt(hi, pb[0]) + nt(hi, pb[1])
+        if lo is not None:
+            a, b = a + nt(lo, far), b + nt(lo, pb[0])
+        a = jnp.sum(a.reshape(n, LEAF, PANEL) * far_pick[None], axis=1)
+        b = jnp.sum(b.reshape(n, LEAF, PANEL) * par_pick[None], axis=1)
+        return a, fold(b)
+
+    low1 = iota((1, 128), 1) < RANK
+
+    def set_pay(step, hi, lo, extra):
+        a, p = coefficients(hi, lo)
+        pay[step, 0:1, :] = a[:, :128]
+        pay[step, 1:2, :] = a[:, 128:]
+        pay[step, 2:3, :] = jnp.where(low1, p, extra)
 
     for k in range(KRY):
         for l in range(k, KRY):
@@ -166,18 +169,28 @@
             gram_rows[8 * k + l : 8 * k + l + 1, :] = r
             if l > k:
                 gram_rows[8 * l + k : 8 * l + k + 1, :] = r
-    set_pay(0, kry[KRY - 1], lanes_of(gram_rows[...], 64))
+    last_hi, last_lo = split(kry[KRY - 1])
+    set_pay(0, last_hi, None, lanes_of(gram_rows[...], 64))
+    halo_src[...] = last_hi
+    vpad[0][LEAF : 2 * LEAF, :] = last_hi.astype(F32)
+    for i in range(LEAF):
+        hi, lo = split(kry[:, i, :])
+        vq[LEAF + i] = jnp.concatenate([hi, lo], axis=0)
 
     pl.semaphore_wait(bar, NROW - 1 + NCOL - 1)
 
+    up = lax.rem(me + 1, NROW)
+    down = lax.rem(me + NROW - 1, NROW)
+
     def send_pay(step):
-        tab[step, me] = pay[step]
-        to_row(lambda p: remote(pay.at[step], tab.at[step, me], pay_s.at[step], pay_r.at[step], (p, col)))
-        up = lax.rem(me + 1, NROW)
-        down = lax.rem(me + NROW - 1, NROW)
-        remote(halo_src.at[step], halo.at[step, 0], halo_s.at[step, 0], halo_r.at[step, 0], (up, col))
-        remote(halo_src.at[step], halo.at[step, 1], halo_s.at[step, 1], halo_r.at[step, 1], (down, col))
-
+        tab[step][me] = pay[step]
+        to_row(lambda p: remote(pay.at[step], tab[step].at[me], pay_s.at[step], pay_r.at[step], (p, col)))
+
+    def to_neighbours(src, low, high, ssem, rsem):
+        remote(src, low, ssem.at[0], rsem.at[0], (up, col))
+        remote(src, high, ssem.at[1], rsem.at[1], (down, col))
+
+    to_neighbours(halo_src, halo.at[0], halo.at[1], halo_s.at[0], halo_r.at[0])
     send_pay(0)
 
     l_fm.wait()
@@ -215,26 +228,56 @@
     for b in range(COARSE):
         fpar[b % 2, 32 + b // 2 : 33 + b // 2, :] = jnp.zeros((1, 128), jnp.int32)
 
+    chip = me // NCORE
+    hi, lo = split(kry[...].reshape(KRY * LEAF, PANEL))
+    a, p = coefficients(hi, lo)
+    qpay[0:KRY, :] = a[:, :128]
+    qpay[KRY : 2 * KRY, :] = a[:, 128:]
+    qpay[2 * KRY :, :] = jnp.where(iota((4, 128), 1) < RANK, p[:4], p[4:])
+    qtab[core, chip, 0:QROWS, :] = qpay[...]
+
+    def to_chip(k, c):
+        peer = far_peer(NCORE * k) // NCORE * NCORE + core
+        remote(qpay, qtab.at[core, chip, pl.ds(0, QROWS)], q_s, q_r, (peer, col))
+        return c
+
+    lax.fori_loop(0, NROW // NCORE - 1, to_chip, 0, unroll=4)
+    own = vq.at[pl.ds(LEAF, LEAF)]
+    to_neighbours(own, vq.at[pl.ds(0, LEAF)], vq.at[pl.ds(2 * LEAF, LEAF)], vq_s, vq_r)
+
     diag = (iota((RANK, PANEL), 0) // LEAF == iota((RANK, PANEL), 1) // RANK).astype(F32)
 
-    def near_part(step):
-        wait(halo.at[step, 0], halo_r.at[step, 0])
-        wait(halo.at[step, 1], halo_r.at[step, 1])
-        vpad[step, 0:LEAF, :] = halo[step, 0].astype(F32)
-        vpad[step, 2 * LEAF :, :] = halo[step, 1].astype(F32)
-
+    def near_at(s, i):
+        return jnp.minimum(lax.rem(nc_s[s, i] - start + LEAF + LEAVES, LEAVES), 3 * LEAF - 1)
+
+    def send_near(step, near):
+        near_src[step] = near
+        near_tab[step, col] = near
+        for k in range(1, NCOL):
+            remote(near_src.at[step], near_tab.at[step, col], near_s.at[step], near_r.at[step], (me, lax.rem(col + k, NCOL)))
+
+    def near_last():
         def body(i, acc):
             out = jnp.zeros((LEAF, PANEL), F32)
             for s in range(2):
-                at = jnp.minimum(lax.rem(nc_s[s, i] - start + LEAF + LEAVES, LEAVES), 3 * LEAF - 1)
-                lhs = jnp.broadcast_to(vpad[step, pl.ds(at, 1), :], (LEAF, PANEL)).astype(BF16)
-                out = out + nt(lhs, nb[i, s])
+                v = jnp.broadcast_to(vpad[0][pl.ds(near_at(s, i), 1), :], (LEAF, PANEL))
+                out = out + nt(v.astype(BF16), nb[i, s])
             return jnp.where(row256 == i, out, acc)
 
-        near_src[step] = lax.fori_loop(0, LEAF, body, jnp.zeros((LEAF, PANEL), F32), unroll=4)
-        near_tab[step, col] = near_src[step]
-        for k in range(1, NCOL):
-            remote(near_src.at[step], near_tab.at[step, col], near_s.at[step], near_r.at[step], (me, lax.rem(col + k, NCOL)))
+        return lax.fori_loop(0, LEAF, body, jnp.zeros((LEAF, PANEL), F32), unroll=16)
+
+    def near_new():
+        def body(i, acc):
+            out = jnp.zeros((2 * LEAF, PANEL), F32)
+            for s in range(2):
+                at = near_at(s, i)
+                v = jnp.broadcast_to(vpad[1][pl.ds(at, 1), :], (LEAF, PANEL))
+                lhs = jnp.where(row256 < 8, v, v - v.astype(BF16).astype(F32)).astype(BF16)
+                out = out + nt(jnp.concatenate([vq[at], lhs], axis=0), nb[i, s])
+            nq[:, pl.ds(i, 1), :] = (out[0:8] + out[8:16]).reshape(KRY, 1, PANEL)
+            return jnp.where(row256 == i, out[16:17] + out[24:25], acc)
+
+        return lax.fori_loop(0, LEAF, body, jnp.zeros((LEAF, PANEL), F32), unroll=16)
 
     def product(t, rows, first):
         xs = []
@@ -249,20 +292,41 @@
         o = o * diag
         return (o[0:16] + o[16:32]) + (o[32:48] + o[48:64])
 
-    def far_part(step):
-        wait(tab.at[step, pl.ds(0, NROW - 1)], pay_r.at[step])
-        for b in range(FAR):
-            c = fc_s[b]
-            grow[b % 2, b // 2 : b // 2 + 1, :] = tab[step, c // LEAF, pl.ds(lax.rem(c, LEAF) // 8, 1), :]
-        for b in range(COARSE):
-            grow[b % 2, 32 + b // 2 : 33 + b // 2, :] = tab[step, cc_s[b] // 4, 2:3, :]
-        low = iota((40, 128), 1) < RANK
-        even, odd = grow[0], grow[1]
-        rows = jnp.where(
-            low,
+    def halves(even, odd):
+        return jnp.where(
+            iota((40, 128), 1) < RANK,
             jnp.where(fpar[0] == 0, even, pltpu.roll(even, 64, 1)),
             jnp.where(fpar[1] == 1, odd, pltpu.roll(odd, 64, 1)),
         )
+
+    def gather(step):
+        for b in range(FAR):
+            c = fc_s[b]
+            grow[b % 2, b // 2 : b // 2 + 1, :] = tab[step][c // LEAF, pl.ds(lax.rem(c, LEAF) // 8, 1), :]
+        for b in range(COARSE):
+            grow[b % 2, 32 + b // 2 : 33 + b // 2, :] = tab[step][cc_s[b] // 4, 2:3, :]
+        return grow[0], grow[1]
+
+    def gather_given():
+        for b in range(FAR):
+            c = fc_s[b]
+            r = c // LEAF
+            second = jnp.full((KRY, 128), lax.rem(c, LEAF), jnp.int32) >= LEAF // 2
+            both = qtab[lax.rem(r, NCORE), r // NCORE, 0 : 2 * KRY, :]
+            qgrow[b % 2, b // 2] = jnp.where(second, both[KRY:], both[:KRY])
+        for b in range(COARSE):
+            r = cc_s[b] // 4
+            pair = qtab[lax.rem(r, NCORE), r // NCORE, 2 * KRY : QROWS, :]
+            turned = pltpu.roll(pair, 64, 1)
+            low = iota((4, 128), 1) < RANK
+            qgrow[b % 2, 32 + b // 2, 0:4, :] = jnp.where(low, pair, turned)
+            qgrow[b % 2, 32 + b // 2, 4:8, :] = jnp.where(low, turned, pair)
+        for k in range(KRY):
+            for p in range(2):
+                qrows[k, p] = qgrow[p, :, k, :]
+
+    def far_part(step, even, odd):
+        rows = halves(even, odd)
         cres = fold(over_groups(product(4, rows, 32)))
         far = product(0, rows, 0) + product(1, rows, 8) + product(2, rows, 16) + product(3, rows, 24)
         hi, lo = split(jnp.concatenate([cres, cres], axis=1) * (lane256 == row256 // 4).astype(F32))
@@ -289,14 +353,10 @@
             base = base + jnp.dot(lhs, cb[4 * g : 4 * g + 4].reshape(4 * RANK, PANEL), preferred_element_type=F32)
         return base
 
-    def exchange(step, row):
-        sc_src[step] = row
-        sc_tab[step, me] = row
-        to_row(lambda p: remote(sc_src.at[step], sc_tab.at[step, me], sc_s.at[step], sc_r.at[step], (p, col)))
-
-    def exchanged(step):
-        wait(sc_tab.at[step, pl.ds(0, NROW - 1)], sc_r.at[step])
-        return jnp.sum(sc_tab[step], axis=0) * (1.0 / COUNT)
+    def exchange(row):
+        sc_src[...] = row
+        sc_tab[me] = row
+        to_row(lambda p: remote(sc_src, sc_tab.at[me], sc_s, sc_r, (p, col)))
 
     lane1 = iota((1, 128), 1)
     sq = (iota((8, 128), 0) == iota((8, 128), 1))
@@ -305,45 +365,70 @@
         return row[:, k : k + 1]
 
     l_nb.wait()
-    near_part(0)
-    far_part(0)
-    gsum = jnp.sum(tab[0], axis=0)[2:3] * (1.0 / COUNT)
+    for j in range(2):
+        wait(halo.at[j], halo_r.at[0, j])
+        vpad[0][2 * LEAF * j : 2 * LEAF * j + LEAF, :] = halo[j].astype(F32)
+    send_near(0, near_last())
+    wait(tab[0].at[pl.ds(0, NROW - 1)], pay_r.at[0])
+    far_part(0, *gather(0))
+    gsum = jnp.sum(tab[0][...], axis=0)[2:3] * (1.0 / COUNT)
     gram = jnp.zeros((8, 128), F32)
     for k in range(KRY):
         gram = jnp.where(iota((8, 128), 0) == k, pltpu.roll(gsum, 64 - 8 * k, 1), gram)
     gram = jnp.where(iota((8, 128), 1) < KRY, gram, 0.0)
     l_sw.wait()
     w = assemble(0, kry[KRY - 1])
-    sums = [partial_sum(kry[k] * w) for k in range(KRY)] + [partial_sum(w * w)]
-    exchange(0, lanes_of(stack_rows(sums, 16), 0))
-    tot = exchanged(0)
 
     def quadratic(tot):
         gh = jnp.sum(gram * tot, axis=1, keepdims=True)
         hcol = jnp.sum(jnp.where(sq, tot, 0.0), axis=1, keepdims=True)
         return jnp.sum(gh * hcol, axis=0, keepdims=True)
 
+    vpad[1][LEAF : 2 * LEAF, :] = w
+    own = vpad[1].at[pl.ds(LEAF, LEAF)]
+    to_neighbours(own, vpad[1].at[pl.ds(0, LEAF)], vpad[1].at[pl.ds(2 * LEAF, LEAF)], halo_s.at[1], halo_r.at[1])
+    sums = [partial_sum(kry[k] * w) for k in range(KRY)] + [partial_sum(w * w)]
+    hi, lo = split(w)
+    set_pay(1, hi, lo, lanes_of(stack_rows(sums, 16), 64))
+    send_pay(1)
+
+    some = qtab.at[core, pl.ds(0, NROW // NCORE - 1), pl.ds(0, QROWS)]
+    half = qtab.at[core, :, pl.ds(0, QROWS)]
+    wait(some, q_r)
+    remote(half, half, qf_s, qf_r, (me + 1 - 2 * core, col))
+    for j in range(2):
+        wait(vpad[1].at[pl.ds(2 * LEAF * j, LEAF)], halo_r.at[1, j])
+        wait(vq.at[pl.ds(2 * LEAF * j, LEAF)], vq_r.at[j])
+    near = near_new()
+    wait(half, qf_r)
+    gather_given()
+
+    wait(tab[1].at[pl.ds(0, NROW - 1)], pay_r.at[1])
+    tot = pltpu.roll(jnp.sum(tab[1][...], axis=0)[2:3], 64, 1) * (1.0 / COUNT)
     h_row = jnp.where(lane1 < KRY, tot, 0.0)
     hh = jnp.sum(h_row * h_row, axis=1, keepdims=True)
     norm = pick(tot, KRY) - 2.0 * hh + quadratic(h_row)
     beta = jnp.sqrt(jnp.maximum(norm, 0.0) + 1e-06)
-    w2 = w
-    for k in range(KRY):
-        w2 = w2 - pick(tot, k) * kry[k]
-    q = w2 / beta
+    inv = 1.0 / beta
+    hs = [pick(tot, k) for k in range(KRY)]
+
+    def less(v, of):
+        for k in range(KRY):
+            v = v - hs[k] * of[k]
+        return v
+
+    send_near(1, less(near, nq) * inv)
+    far_part(1, *[less(g, qrows.at[:, p]) * inv for p, g in enumerate(gather(1))])
+    q = less(w, kry) / beta
     out_v[0] = q
     line = jnp.where(lane1 == KRY + 1, beta, h_row)
     out_h[0:1, :] = line[:, : KRY + 2]
-
-    set_pay(1, q, None)
-    send_pay(1)
     new_gram = [partial_sum(kry[k] * q) for k in range(KRY)] + [partial_sum(q * q)]
-    near_part(1)
-    far_part(1)
     w = assemble(1, q)
     sums = [partial_sum(kry[k] * w) for k in range(KRY)] + [partial_sum(q * w), partial_sum(w * w)]
-    exchange(1, lanes_of(stack_rows(sums + [jnp.zeros((1, 128), F32)] * 6 + new_gram, 32), 0))
-    tot = exchanged(1)
+    exchange(lanes_of(stack_rows(sums + [jnp.zeros((1, 128), F32)] * 6 + new_gram, 32), 0))
+    wait(sc_tab.at[pl.ds(0, NROW - 1)], sc_r)
+    tot = jnp.sum(sc_tab[...], axis=0) * (1.0 / COUNT)
     h_all = jnp.where(lane1 <= KRY, tot, 0.0)
     h_row = jnp.where(lane1 < KRY, tot, 0.0)
     g_row = jnp.where(lane1 <= KRY, pltpu.roll(tot, 128 - 16, 1), 0.0)
@@ -360,12 +445,21 @@
     out_h[1:2, :] = line[:, : KRY + 2]
 
     for step in range(2):
-        wait(tab.at[step, pl.ds(0, NROW - 1)], pay_s.at[step])
-        wait(halo.at[step, 0], halo_s.at[step, 0])
-        wait(halo.at[step, 1], halo_s.at[step, 1])
+        wait(tab[step].at[pl.ds(0, NROW - 1)], pay_s.at[step])
         wait(near_tab.at[step, pl.ds(0, NCOL - 1)], near_s.at[step])
         wait(far_tab.at[step, pl.ds(0, NCOL - 1)], far_s.at[step])
-        wait(sc_tab.at[step, pl.ds(0, NROW - 1)], sc_s.at[step])
+    for j in range(2):
+        wait(halo.at[j], halo_s.at[0, j])
+        wait(vpad[1].at[pl.ds(LEAF, LEAF)], halo_s.at[1, j])
+        wait(vq.at[pl.ds(LEAF, LEAF)], vq_s.at[j])
+    wait(sc_tab.at[pl.ds(0, NROW - 1)], sc_s)
+    wait(some, q_s)
+    wait(half, qf_s)
+
+
+def copy_out(v_in, h_in, v_out, h_out):
+    v_out[...] = v_in[...]
+    h_out[...] = h_in[...]
 
 
 def shards(krylov, self_weight, cluster_basis, transfer, near_blocks, near_cols, far_row, far_col, far_mat, coarse_row, coarse_col, coarse_mat):
@@ -374,12 +468,10 @@
     vmem = pl.BlockSpec(memory_space=pltpu.VMEM)
     V = pltpu.VMEM
     DMA = pltpu.SemaphoreType.DMA
-    return pl.pallas_call(
+    shapes = (jax.ShapeDtypeStruct((2, LEAF, PANEL), F32), jax.ShapeDtypeStruct((2, KRY + 2), F32))
+    vectors, hessen = pl.pallas_call(
         kernel,
-        out_shape=(
-            jax.ShapeDtypeStruct((2, LEAF, PANEL), F32),
-            jax.ShapeDtypeStruct((2, KRY + 2), F32),
-        ),
+        out_shape=shapes,
         in_specs=[anywhere] * 12,
         out_specs=(vmem, vmem),
         scratch_shapes=[
@@ -399,23 +491,32 @@
             V((2, 40, 128), jnp.int32),
             V((64, 128), F32),
             V((2, 3, 128), F32),
-            V((2, NROW, 3, 128), F32),
+            V((NROW, 3, 128), F32),
+            V((NROW, 3, 128), F32),
+            V((LEAF, PANEL), BF16),
             V((2, LEAF, PANEL), BF16),
-            V((2, 2, LEAF, PANEL), BF16),
-            V((2, 3 * LEAF, PANEL), F32),
+            V((3 * LEAF, 2 * KRY, PANEL), BF16),
+            V((3 * LEAF, PANEL), F32),
+            V((3 * LEAF, PANEL), F32),
+            V((KRY, LEAF, PANEL), F32),
+            V((QROWS, 128), F32),
+            V((NCORE, NROW // NCORE, 24, 128), F32),
+            V((2, 40, KRY, 128), F32),
+            V((KRY, 2, 40, 128), F32),
             V((2, 40, 128), F32),
             V((2, LEAF, PANEL), F32),
             V((2, NCOL, LEAF, PANEL), F32),
             V((2, 8, 128), F32),
             V((2, NCOL, 8, 128), F32),
-            V((2, 1, 128), F32),
-            V((2, NROW, 1, 128), F32),
+            V((1, 128), F32),
+            V((NROW, 1, 128), F32),
             DMA((16,)),
             DMA((2,)), DMA((2,)),
             DMA((2, 2)), DMA((2, 2)),
             DMA((2,)), DMA((2,)),
             DMA((2,)), DMA((2,)),
-            DMA((2,)), DMA((2,)),
+            DMA(()), DMA(()),
+            DMA(()), DMA(()), DMA(()), DMA(()), DMA((2,)), DMA((2,)),
         ],
         compiler_params=pltpu.CompilerParams(
             collective_id=0, has_side_effects=True, vmem_limit_bytes=60 * 2**20
@@ -435,6 +536,14 @@
         coarse_row.reshape(COARSE),
         coarse_col.reshape(COARSE),
     )
+    return pl.pallas_call(
+        copy_out,
+        out_shape=shapes,
+        in_specs=[vmem] * 2,
+        out_specs=(vmem, vmem),
+        compiler_params=pltpu.CompilerParams(vmem_limit_bytes=60 * 2**20),
+        name="results",
+    )(vectors, hessen)
 
 
 def solution(mesh):

time: 51.8 us -> 44.7 us (0.86)
  Pallas kernels: 48.4 us -> 43.9 us
  local copies, waits for them, and re-layouts: 2.6 us -> 0 us
    pallas_call x1 -> x2, Pallas kernels: 48.4 us -> 43.9 us  [the longest x1 42.5 us: shards(): pl.pallas_call(kernel, out_shape=shapes, in_specs=[anywhere] * 12, out_sp...]
    unnamed x2 -> x0, local copies, waits for them, and re-layouts: 2.6 us -> none
where the time goes in v2:
time: 44.7 us; the launch traced here: 44.6 us
  Pallas kernels  43.9 us (98%)
  between operations  0.64 us (1%)
    pallas_call x1, Pallas kernels, shards(): pl.pallas_call(kernel, out_shape=shapes, in_specs=[anywhere] * 12, out_sp...  42.5 us
    pallas_call x1, Pallas kernels, shards(): pl.pallas_call(copy_out, out_shape=shapes, in_specs=[vmem] * 2, out_specs...  1.38 us

profile of v2, /device:TPU:1, one launch (start us, length us, event | category | flops | bytes accessed | tf_op | source)
XLA Modules:
  0.0 44.6 jit_solution(15463692261167161570)
XLA Ops:
  0.6 42.5 %hmatrix_gmres.1 = (f32[2,16,256]{2,1,0:T(8,128)}, f32[2,10]{1,0:T(2,128)}) custom-call(f32[8,16,256]{2,1,0:T(8,128)} %kry_h.1, f32[16,256]{1,0:T(8,128)} %sw_h.1, bf16[16,64,256]{2,1,0:T(8,128)(2,1)} %cb_h.1, f32[16,64,64]{2,1,0:T(8,128)} %tr_h.1, bf16[16,2,256,256]{3,2,1,0:T(8,128)(2,1)} %nb_h.1, f32[64,64,64]{2,1,0:T(8,128)} %bitcast.7, ...), custom_call_target="tpu_custom_call" | custom-call | tf_op jit(solution)/shard_map/hmatrix_gmres/pallas_call | solution.py:472
  43.2 1.4 %results.1 = (f32[2,16,256]{2,1,0:T(8,128)}, f32[2,10]{1,0:T(2,128)}) custom-call(f32[2,16,256]{2,1,0:T(8,128)} %get-tuple-element.4.v_in, f32[2,10]{1,0:T(2,128)} %get-tuple-element.5.h_in), custom_call_target="tpu_custom_call" | custom-call | tf_op jit(solution)/shard_map/results/pallas_call | solution.py:539

commit v3 on v2

--- a/solution.py
+++ b/solution.py
@@ -16,7 +16,7 @@
 LEAF, PANEL, RANK, KRY = 16, 256, 64, 8
 LEAVES = NROW * LEAF
 FAR, COARSE = 64, 16
-QROWS = 20
+QROWS = 21
 COUNT = float(LEAVES * PANEL)
 
 
@@ -49,21 +49,34 @@
     return jnp.sum(jnp.where(iota((n, 128), 1) == iota((n, 128), 0) + first, sums, 0.0), axis=0, keepdims=True)
 
 
-def stack_rows(rows, n):
-    out = jnp.zeros((n, 128), F32)
-    at = iota((n, 128), 0)
-    for j, r in enumerate(rows):
-        out = jnp.where(at == j, r, out)
-    return out
+def totals(pairs):
+    eights = []
+    for x, _ in pairs:
+        s = x[:8] + x[8:]
+        eights.append(s[:, :128] + s[:, 128:])
+    sums = jnp.sum(jnp.concatenate(eights, axis=0), axis=1, keepdims=True)
+    lane = iota((8, 128), 1)
+    out = jnp.zeros((8, 128), F32)
+    for j, (_, at) in enumerate(pairs):
+        out = jnp.where(lane == at, sums[8 * j : 8 * j + 8], out)
+    return jnp.sum(out, axis=0, keepdims=True)
+
+
+def tree(x):
+    n = x.shape[0]
+    while n > 1:
+        n //= 2
+        x = x[:n] + x[n:]
+    return x[0]
 
 
 def kernel(
     kry_h, sw_h, cb_h, tr_h, nb_h, fm_h, cm_h, nc_h, fr_h, fc_h, cr_h, cc_h,
     out_v, out_h,
-    nc_s, fr_s, fc_s, cr_s, cc_s,
+    nc_s, fr_s, fc_s, cr_s, cc_s, row_s, half_s,
     kry, sw, cb, bfar, tr, nb, fm, cm,
-    pb, ftile, ttile, fmask, fpar, gram_rows,
-    pay, tab_a, tab_b, halo_src, halo, vq, vpad_a, vpad_b, nq, qpay, qtab, qgrow, qrows, grow, near_src, near_tab, far_src, far_tab, sc_src, sc_tab,
+    pb, ftile, ttile, fmask, adds_to, fpar, gram_rows,
+    pay, tab_a, tab_b, halo_src, halo, vq, vpad_a, vpad_b, nq, qpay, qtab, qgrow, qrows, grow, near_src_a, near_src_b, near_tab_a, near_tab_b, far_src, far_tab, sc_src, sc_tab,
     load_sem, pay_s, pay_r, halo_s, halo_r, near_s, near_r, far_s, far_r, sc_s, sc_r, q_s, q_r, qf_s, qf_r, vq_s, vq_r,
 ):
     tab, vpad = (tab_a, tab_b), (vpad_a, vpad_b)
@@ -73,24 +86,6 @@
     z = lax.rem(me // NCORE, NZ)
     core = lax.rem(me, NCORE)
     start = me * LEAF
-
-    loads = []
-
-    def load(src, dst):
-        c = pltpu.make_async_copy(src, dst, load_sem.at[len(loads)])
-        c.start()
-        loads.append(c)
-        return c
-
-    l_kry = load(kry_h, kry)
-    l_cb = load(cb_h, cb)
-    l_bf = [load(cb_h.at[4 * k + col], bfar.at[k]) for k in range(4)]
-    l_tr = load(tr_h, tr)
-    l_fm = load(fm_h, fm)
-    l_cm = load(cm_h, cm)
-    l_nb = load(nb_h, nb)
-    l_sw = load(sw_h, sw)
-    l_index = [load(h, s) for h, s in ((nc_h, nc_s), (fr_h, fr_s), (fc_h, fc_s), (cr_h, cr_s), (cc_h, cc_s))]
 
     bar = pltpu.get_barrier_semaphore()
 
@@ -116,6 +111,18 @@
     for k in range(1, NCOL):
         pl.semaphore_signal(bar, inc=1, device_id=(me, lax.rem(col + k, NCOL)), device_id_type=MESH)
 
+    loads = []
+
+    def load(src, dst):
+        c = pltpu.make_async_copy(src, dst, load_sem.at[len(loads)])
+        c.start()
+        loads.append(c)
+        return c
+
+    l_kry = load(kry_h, kry)
+    l_cb = load(cb_h, cb)
+    l_bf = [load(cb_h.at[4 * k + col], bfar.at[k]) for k in range(4)]
+    l_tr = load(tr_h, tr)
     def remote(src, dst, ssem, rsem, dev):
         pltpu.make_async_remote_copy(
             src_ref=src, dst_ref=dst, send_sem=ssem, recv_sem=rsem, device_id=dev, device_id_type=MESH
@@ -132,15 +139,18 @@
     l_tr.wait()
     for k in range(4):
         child = 4 * col + k
-        prod = lax.dot_general(
-            tr[child], cb[child].astype(F32), (((0,), (0,)), ((), ())),
-            precision=lax.Precision.HIGHEST, preferred_element_type=F32,
-        )
-        hi, lo = split(prod)
+        terms = jnp.concatenate(split(tr[child].T), axis=0)
+        prod = jnp.dot(terms, cb[child], preferred_element_type=F32)
+        hi, lo = split(prod[:RANK] + prod[RANK:])
         pb[0, RANK * k : RANK * (k + 1), :] = hi
         pb[1, RANK * k : RANK * (k + 1), :] = lo
     for c in l_bf:
         c.wait()
+    l_index = [load(h, s) for h, s in ((nc_h, nc_s), (fr_h, fr_s), (fc_h, fc_s), (cr_h, cr_s), (cc_h, cc_s))]
+    l_fm = load(fm_h, fm)
+    l_cm = load(cm_h, cm)
+    l_nb = load(nb_h, nb)
+    l_sw = load(sw_h, sw)
 
     far_pick = (row256 == 4 * lane256 + col).astype(F32)
     par_pick = (row256 == 4 * col + lane256).astype(F32)
@@ -163,36 +173,54 @@
         pay[step, 1:2, :] = a[:, 128:]
         pay[step, 2:3, :] = jnp.where(low1, p, extra)
 
+    last_hi = kry[KRY - 1].astype(BF16)
+    set_pay(0, last_hi, None, jnp.zeros((1, 128), F32))
+    halo_src[...] = last_hi
+    vpad[0][LEAF : 2 * LEAF, :] = last_hi.astype(F32)
+    for i in range(LEAF):
+        hi, lo = split(kry[:, i, :])
+        vq[LEAF + i] = jnp.concatenate([hi, lo], axis=0)
+
+    pl.semaphore_wait(bar, NROW - 1 + NCOL - 1)
+
+    up = lax.rem(me + 1, NROW)
+    down = lax.rem(me + NROW - 1, NROW)
+
+    def send_pay(step):
+        tab[step][me] = pay[step]
+        to_row(lambda p: remote(pay.at[step], tab[step].at[me], pay_s.at[step], pay_r.at[step], (p, col)))
+
+    def to_neighbours(src, low, high, ssem, rsem):
+        remote(src, low, ssem.at[0], rsem.at[0], (up, col))
+        remote(src, high, ssem.at[1], rsem.at[1], (down, col))
+
+    to_neighbours(halo_src, halo.at[0], halo.at[1], halo_s.at[0], halo_r.at[0])
+    send_pay(0)
+
+    own = vq.at[pl.ds(LEAF, LEAF)]
+    to_neighbours(own, vq.at[pl.ds(0, LEAF)], vq.at[pl.ds(2 * LEAF, LEAF)], vq_s, vq_r)
+
     for k in range(KRY):
         for l in range(k, KRY):
             r = partial_sum(kry[k] * kry[l])
             gram_rows[8 * k + l : 8 * k + l + 1, :] = r
             if l > k:
                 gram_rows[8 * l + k : 8 * l + k + 1, :] = r
-    last_hi, last_lo = split(kry[KRY - 1])
-    set_pay(0, last_hi, None, lanes_of(gram_rows[...], 64))
-    halo_src[...] = last_hi
-    vpad[0][LEAF : 2 * LEAF, :] = last_hi.astype(F32)
-    for i in range(LEAF):
-        hi, lo = split(kry[:, i, :])
-        vq[LEAF + i] = jnp.concatenate([hi, lo], axis=0)
-
-    pl.semaphore_wait(bar, NROW - 1 + NCOL - 1)
-
-    up = lax.rem(me + 1, NROW)
-    down = lax.rem(me + NROW - 1, NROW)
-
-    def send_pay(step):
-        tab[step][me] = pay[step]
-        to_row(lambda p: remote(pay.at[step], tab[step].at[me], pay_s.at[step], pay_r.at[step], (p, col)))
-
-    def to_neighbours(src, low, high, ssem, rsem):
-        remote(src, low, ssem.at[0], rsem.at[0], (up, col))
-        remote(src, high, ssem.at[1], rsem.at[1], (down, col))
-
-    to_neighbours(halo_src, halo.at[0], halo.at[1], halo_s.at[0], halo_r.at[0])
-    send_pay(0)
-
+    chip = me // NCORE
+    hi, lo = split(kry[...].reshape(KRY * LEAF, PANEL))
+    a, p = coefficients(hi, lo)
+    qpay[0:KRY, :] = a[:, :128]
+    qpay[KRY : 2 * KRY, :] = a[:, 128:]
+    qpay[QROWS - 1 :, :] = lanes_of(gram_rows[...], 64)
+    qpay[2 * KRY : QROWS - 1, :] = jnp.where(iota((4, 128), 1) < RANK, p[:4], p[4:])
+    qtab[core, chip, 0:QROWS, :] = qpay[...]
+
+    def to_chip(k, c):
+        peer = far_peer(NCORE * k) // NCORE * NCORE + core
+        remote(qpay, qtab.at[core, chip, pl.ds(0, QROWS)], q_s, q_r, (peer, col))
+        return c
+
+    lax.fori_loop(0, NROW // NCORE - 1, to_chip, 0, unroll=4)
     l_fm.wait()
     l_cm.wait()
     for c in l_index:
@@ -211,50 +239,43 @@
         ttile[0, RANK * j : RANK * (j + 1), :] = hi
         ttile[1, RANK * j : RANK * (j + 1), :] = lo
 
-    for t in range(5):
-        for n in range(4):
-            row = jnp.zeros((LEAF, PANEL), jnp.int32)
-            for k in range(4):
-                if t < 4:
-                    at = fr_s[16 * t + 4 * n + k] - start
-                else:
-                    at = cr_s[4 * n + k] - 4 * me
-                row = jnp.where(lane256 == k, at, row)
-            mine = row256 if t < 4 else row256 // 4
-            fmask[t, LEAF * n : LEAF * (n + 1), :] = (row == mine).astype(F32)
+    for n in range(4):
+        row = jnp.zeros((LEAF, PANEL), jnp.int32)
+        for k in range(4):
+            row = jnp.where(lane256 == k, cr_s[4 * n + k] - 4 * me, row)
+        fmask[LEAF * n : LEAF * (n + 1), :] = (row == row256 // 4).astype(F32)
+    at = iota((LEAF, FAR), 1)
+    row = jnp.zeros((LEAF, FAR), jnp.int32)
+    for t in range(4):
+        for odd in range(2):
+            for n in range(4):
+                for pair in range(2):
+                    row = jnp.where(at == 16 * t + 8 * odd + 2 * n + pair, fr_s[16 * t + 4 * n + 2 * pair + odd] - start, row)
+    adds = (row == iota((LEAF, FAR), 0)).astype(F32)
+    adds_to[...] = jnp.concatenate([adds, adds], axis=1).astype(BF16)
     for b in range(FAR):
-        half = lax.rem(fc_s[b] // 4, 2)
+        within = lax.rem(fc_s[b], LEAF)
+        row_s[b] = fc_s[b] // LEAF
+        half_s[b] = within // 8
+        half = lax.rem(within // 4, 2)
         fpar[b % 2, b // 2 : b // 2 + 1, :] = jnp.full((1, 128), half, jnp.int32)
     for b in range(COARSE):
+        row_s[FAR + b] = cc_s[b] // 4
         fpar[b % 2, 32 + b // 2 : 33 + b // 2, :] = jnp.zeros((1, 128), jnp.int32)
-
-    chip = me // NCORE
-    hi, lo = split(kry[...].reshape(KRY * LEAF, PANEL))
-    a, p = coefficients(hi, lo)
-    qpay[0:KRY, :] = a[:, :128]
-    qpay[KRY : 2 * KRY, :] = a[:, 128:]
-    qpay[2 * KRY :, :] = jnp.where(iota((4, 128), 1) < RANK, p[:4], p[4:])
-    qtab[core, chip, 0:QROWS, :] = qpay[...]
-
-    def to_chip(k, c):
-        peer = far_peer(NCORE * k) // NCORE * NCORE + core
-        remote(qpay, qtab.at[core, chip, pl.ds(0, QROWS)], q_s, q_r, (peer, col))
-        return c
-
-    lax.fori_loop(0, NROW // NCORE - 1, to_chip, 0, unroll=4)
-    own = vq.at[pl.ds(LEAF, LEAF)]
-    to_neighbours(own, vq.at[pl.ds(0, LEAF)], vq.at[pl.ds(2 * LEAF, LEAF)], vq_s, vq_r)
 
     diag = (iota((RANK, PANEL), 0) // LEAF == iota((RANK, PANEL), 1) // RANK).astype(F32)
 
     def near_at(s, i):
         return jnp.minimum(lax.rem(nc_s[s, i] - start + LEAF + LEAVES, LEAVES), 3 * LEAF - 1)
 
+    near_src, near_tab = (near_src_a, near_src_b), (near_tab_a, near_tab_b)
+
     def send_near(step, near):
-        near_src[step] = near
-        near_tab[step, col] = near
+        src, held = near_src[step], near_tab[step]
+        src[...] = near.astype(src.dtype)
+        held[col] = src[...]
         for k in range(1, NCOL):
-            remote(near_src.at[step], near_tab.at[step, col], near_s.at[step], near_r.at[step], (me, lax.rem(col + k, NCOL)))
+            remote(src, held.at[col], near_s.at[step], near_r.at[step], (me, lax.rem(col + k, NCOL)))
 
     def near_last():
         def body(i, acc):
@@ -284,9 +305,20 @@
         for n in range(4):
             r = jnp.concatenate([rows[first + 2 * n : first + 2 * n + 1], rows[first + 2 * n + 1 : first + 2 * n + 2]], axis=1)
             xs.append(jnp.broadcast_to(r, (LEAF, PANEL)))
-        hi, lo = split(jnp.concatenate(xs, axis=0) * fmask[t])
+        hi, lo = split(jnp.concatenate(xs, axis=0) * fmask[...])
         o = nt(jnp.concatenate([hi, lo], axis=0), ftile[t, 0])
         return o[:RANK] + o[RANK:] + nt(hi, ftile[t, 1])
+
+    row16, lane128 = iota((LEAF, 128), 0), iota((LEAF, 128), 1)
+    own_half = ((row16 // 8) == (lane128 // RANK)).astype(F32)
+    own_pair = [own_half * (lax.rem(row16, 2) == j).astype(F32) for j in range(2)]
+    own_group = (lax.rem(row256, 8) // 2 == lane256).astype(F32)
+
+    def block_results(t, rows):
+        both = jnp.concatenate([rows, rows], axis=0)
+        hi, lo = split(jnp.concatenate([both * own_pair[0], both * own_pair[1]], axis=1))
+        o = nt(jnp.concatenate([hi, lo], axis=0), ftile[t, 0])
+        return fold((o[:LEAF] + o[LEAF:] + nt(hi, ftile[t, 1])) * own_group)
 
     def over_groups(o):
         o = o * diag
@@ -301,22 +333,20 @@
 
     def gather(step):
         for b in range(FAR):
-            c = fc_s[b]
-            grow[b % 2, b // 2 : b // 2 + 1, :] = tab[step][c // LEAF, pl.ds(lax.rem(c, LEAF) // 8, 1), :]
+            grow[b % 2, b // 2 : b // 2 + 1, :] = tab[step][row_s[b], pl.ds(half_s[b], 1), :]
         for b in range(COARSE):
-            grow[b % 2, 32 + b // 2 : 33 + b // 2, :] = tab[step][cc_s[b] // 4, 2:3, :]
+            grow[b % 2, 32 + b // 2 : 33 + b // 2, :] = tab[step][row_s[FAR + b], 2:3, :]
         return grow[0], grow[1]
 
     def gather_given():
         for b in range(FAR):
-            c = fc_s[b]
-            r = c // LEAF
-            second = jnp.full((KRY, 128), lax.rem(c, LEAF), jnp.int32) >= LEAF // 2
+            r = row_s[b]
+            second = jnp.full((KRY, 128), half_s[b], jnp.int32) == 1
             both = qtab[lax.rem(r, NCORE), r // NCORE, 0 : 2 * KRY, :]
             qgrow[b % 2, b // 2] = jnp.where(second, both[KRY:], both[:KRY])
         for b in range(COARSE):
-            r = cc_s[b] // 4
-            pair = qtab[lax.rem(r, NCORE), r // NCORE, 2 * KRY : QROWS, :]
+            r = row_s[FAR + b]
+            pair = qtab[lax.rem(r, NCORE), r // NCORE, 2 * KRY : QROWS - 1, :]
             turned = pltpu.roll(pair, 64, 1)
             low = iota((4, 128), 1) < RANK
             qgrow[b % 2, 32 + b // 2, 0:4, :] = jnp.where(low, pair, turned)
@@ -328,30 +358,35 @@
     def far_part(step, even, odd):
         rows = halves(even, odd)
         cres = fold(over_groups(product(4, rows, 32)))
-        far = product(0, rows, 0) + product(1, rows, 8) + product(2, rows, 16) + product(3, rows, 24)
+        blocks = jnp.concatenate([block_results(t, rows[8 * t : 8 * t + 8]) for t in range(4)], axis=0)
+        far = jnp.dot(adds_to[...], jnp.concatenate(split(blocks), axis=0), preferred_element_type=F32)
         hi, lo = split(jnp.concatenate([cres, cres], axis=1) * (lane256 == row256 // 4).astype(F32))
         o = nt(jnp.concatenate([hi, lo], axis=0), ttile[0])
         down = o[:LEAF] + o[LEAF:] + nt(hi, ttile[1])
-        total = fold(over_groups(far) + down * (lane256 == lax.rem(row256, 4)).astype(F32))
+        total = far + fold(down * (lane256 == lax.rem(row256, 4)).astype(F32))
         far_src[step] = jnp.where(iota((8, 128), 1) < RANK, total[:8], total[8:])
         far_tab[step, col] = far_src[step]
         for k in range(1, NCOL):
             remote(far_src.at[step], far_tab.at[step, col], far_s.at[step], far_r.at[step], (me, lax.rem(col + k, NCOL)))
 
-    def assemble(step, v):
-        wait(near_tab.at[step, pl.ds(0, NCOL - 1)], near_r.at[step])
-        near = (near_tab[step, 0] + near_tab[step, 1]) + (near_tab[step, 2] + near_tab[step, 3])
+    back_mask = jnp.concatenate([(row256 == 4 * g + lane256).astype(F32) for g in range(4)], axis=1)
+
+    def assemble(step, v, scale):
+        wait(near_tab[step].at[pl.ds(0, NCOL - 1)], near_r.at[step])
+        parts = [near_tab[step][c].astype(F32) for c in range(NCOL)]
+        near = (parts[0] + parts[1]) + (parts[2] + parts[3])
+        if scale is not None:
+            near = near * scale
         base = sw[...] * v + near
         wait(far_tab.at[step, pl.ds(0, NCOL - 1)], far_r.at[step])
         far = (far_tab[step, 0] + far_tab[step, 1]) + (far_tab[step, 2] + far_tab[step, 3])
+        if scale is not None:
+            far = far * scale
         back = pltpu.roll(far, 64, 1)
         low = iota((8, 128), 1) < RANK
         both = jnp.concatenate([jnp.where(low, far, back), jnp.where(low, back, far)], axis=0)
-        both = jnp.concatenate([both, both], axis=1).astype(BF16).astype(F32)
-        for g in range(4):
-            lhs = jnp.where(row256 == 4 * g + lane256, both, 0.0).astype(BF16)
-            base = base + jnp.dot(lhs, cb[4 * g : 4 * g + 4].reshape(4 * RANK, PANEL), preferred_element_type=F32)
-        return base
+        lhs = (jnp.concatenate([both] * 8, axis=1) * back_mask).astype(BF16)
+        return base + jnp.dot(lhs, cb[...].reshape(LEAF * RANK, PANEL), preferred_element_type=F32)
 
     def exchange(row):
         sc_src[...] = row
@@ -371,13 +406,8 @@
     send_near(0, near_last())
     wait(tab[0].at[pl.ds(0, NROW - 1)], pay_r.at[0])
     far_part(0, *gather(0))
-    gsum = jnp.sum(tab[0][...], axis=0)[2:3] * (1.0 / COUNT)
-    gram = jnp.zeros((8, 128), F32)
-    for k in range(KRY):
-        gram = jnp.where(iota((8, 128), 0) == k, pltpu.roll(gsum, 64 - 8 * k, 1), gram)
-    gram = jnp.where(iota((8, 128), 1) < KRY, gram, 0.0)
     l_sw.wait()
-    w = assemble(0, kry[KRY - 1])
+    w = assemble(0, kry[KRY - 1], None)
 
     def quadratic(tot):
         gh = jnp.sum(gram * tot, axis=1, keepdims=True)
@@ -387,9 +417,8 @@
     vpad[1][LEAF : 2 * LEAF, :] = w
     own = vpad[1].at[pl.ds(LEAF, LEAF)]
     to_neighbours(own, vpad[1].at[pl.ds(0, LEAF)], vpad[1].at[pl.ds(2 * LEAF, LEAF)], halo_s.at[1], halo_r.at[1])
-    sums = [partial_sum(kry[k] * w) for k in range(KRY)] + [partial_sum(w * w)]
     hi, lo = split(w)
-    set_pay(1, hi, lo, lanes_of(stack_rows(sums, 16), 64))
+    set_pay(1, hi, lo, totals([(kry[k] * w, RANK + k) for k in range(KRY)] + [(w * w, RANK + KRY)]))
     send_pay(1)
 
     some = qtab.at[core, pl.ds(0, NROW // NCORE - 1), pl.ds(0, QROWS)]
@@ -402,9 +431,14 @@
     near = near_new()
     wait(half, qf_r)
     gather_given()
+    gsum = jnp.sum(qtab[:, :, QROWS - 1 : QROWS, :].reshape(NROW, 1, 128), axis=0) * (1.0 / COUNT)
+    gram = jnp.zeros((8, 128), F32)
+    for k in range(KRY):
+        gram = jnp.where(iota((8, 128), 0) == k, pltpu.roll(gsum, 64 - 8 * k, 1), gram)
+    gram = jnp.where(iota((8, 128), 1) < KRY, gram, 0.0)
 
     wait(tab[1].at[pl.ds(0, NROW - 1)], pay_r.at[1])
-    tot = pltpu.roll(jnp.sum(tab[1][...], axis=0)[2:3], 64, 1) * (1.0 / COUNT)
+    tot = pltpu.roll(tree(tab[1][...])[2:3], 64, 1) * (1.0 / COUNT)
     h_row = jnp.where(lane1 < KRY, tot, 0.0)
     hh = jnp.sum(h_row * h_row, axis=1, keepdims=True)
     norm = pick(tot, KRY) - 2.0 * hh + quadratic(h_row)
@@ -417,18 +451,17 @@
             v = v - hs[k] * of[k]
         return v
 
-    send_near(1, less(near, nq) * inv)
-    far_part(1, *[less(g, qrows.at[:, p]) * inv for p, g in enumerate(gather(1))])
-    q = less(w, kry) / beta
+    send_near(1, less(near, nq))
+    far_part(1, *[less(g, qrows.at[:, p]) for p, g in enumerate(gather(1))])
+    q = less(w, kry) * inv
     out_v[0] = q
     line = jnp.where(lane1 == KRY + 1, beta, h_row)
     out_h[0:1, :] = line[:, : KRY + 2]
-    new_gram = [partial_sum(kry[k] * q) for k in range(KRY)] + [partial_sum(q * q)]
-    w = assemble(1, q)
-    sums = [partial_sum(kry[k] * w) for k in range(KRY)] + [partial_sum(q * w), partial_sum(w * w)]
-    exchange(lanes_of(stack_rows(sums + [jnp.zeros((1, 128), F32)] * 6 + new_gram, 32), 0))
+    new_gram = totals([(kry[k] * q, 16 + k) for k in range(KRY)] + [(q * q, 16 + KRY)])
+    w = assemble(1, q, inv)
+    exchange(new_gram + totals([(kry[k] * w, k) for k in range(KRY)] + [(q * w, KRY), (w * w, KRY + 1)]))
     wait(sc_tab.at[pl.ds(0, NROW - 1)], sc_r)
-    tot = jnp.sum(sc_tab[...], axis=0) * (1.0 / COUNT)
+    tot = tree(sc_tab[...]) * (1.0 / COUNT)
     h_all = jnp.where(lane1 <= KRY, tot, 0.0)
     h_row = jnp.where(lane1 < KRY, tot, 0.0)
     g_row = jnp.where(lane1 <= KRY, pltpu.roll(tot, 128 - 16, 1), 0.0)
@@ -440,13 +473,13 @@
     w2 = w - h8 * q
     for k in range(KRY):
         w2 = w2 - pick(tot, k) * kry[k]
-    out_v[1] = w2 / beta
+    out_v[1] = w2 * (1.0 / beta)
     line = jnp.where(lane1 == KRY + 1, beta, h_all)
     out_h[1:2, :] = line[:, : KRY + 2]
 
     for step in range(2):
         wait(tab[step].at[pl.ds(0, NROW - 1)], pay_s.at[step])
-        wait(near_tab.at[step, pl.ds(0, NCOL - 1)], near_s.at[step])
+        wait(near_tab[step].at[pl.ds(0, NCOL - 1)], near_s.at[step])
         wait(far_tab.at[step, pl.ds(0, NCOL - 1)], far_s.at[step])
     for j in range(2):
         wait(halo.at[j], halo_s.at[0, j])
@@ -457,9 +490,12 @@
     wait(half, qf_s)
 
 
-def copy_out(v_in, h_in, v_out, h_out):
-    v_out[...] = v_in[...]
-    h_out[...] = h_in[...]
+def copy_out(v_in, h_in, v_out, h_out, sem):
+    copies = [pltpu.make_async_copy(v_in, v_out, sem.at[0]), pltpu.make_async_copy(h_in, h_out, sem.at[1])]
+    for c in copies:
+        c.start()
+    for c in copies:
+        c.wait()
 
 
 def shards(krylov, self_weight, cluster_basis, transfer, near_blocks, near_cols, far_row, far_col, far_mat, coarse_row, coarse_col, coarse_mat):
@@ -471,11 +507,12 @@
     shapes = (jax.ShapeDtypeStruct((2, LEAF, PANEL), F32), jax.ShapeDtypeStruct((2, KRY + 2), F32))
     vectors, hessen = pl.pallas_call(
         kernel,
-        out_shape=shapes,
+        out_shape=(V((2, LEAF, PANEL), F32), V((2, KRY + 2), F32)),
         in_specs=[anywhere] * 12,
         out_specs=(vmem, vmem),
         scratch_shapes=[
             S((2, LEAF), jnp.int32), S((FAR,), jnp.int32), S((FAR,), jnp.int32), S((COARSE,), jnp.int32), S((COARSE,), jnp.int32),
+            S((FAR + COARSE,), jnp.int32), S((FAR,), jnp.int32),
             V((KRY, LEAF, PANEL), F32),
             V((LEAF, PANEL), F32),
             V((LEAF, RANK, PANEL), BF16),
@@ -487,7 +524,8 @@
             V((2, 4 * RANK, PANEL), BF16),
             V((5, 2, 4 * RANK, 4 * RANK), BF16),
             V((2, 4 * RANK, 4 * RANK), BF16),
-            V((5, 4 * LEAF, 4 * RANK), F32),
+            V((4 * LEAF, 4 * RANK), F32),
+            V((LEAF, 2 * FAR), BF16),
             V((2, 40, 128), jnp.int32),
             V((64, 128), F32),
             V((2, 3, 128), F32),
@@ -504,8 +542,10 @@
             V((2, 40, KRY, 128), F32),
             V((KRY, 2, 40, 128), F32),
             V((2, 40, 128), F32),
-            V((2, LEAF, PANEL), F32),
-            V((2, NCOL, LEAF, PANEL), F32),
+            V((LEAF, PANEL), F32),
+            V((LEAF, PANEL), BF16),
+            V((NCOL, LEAF, PANEL), F32),
+            V((NCOL, LEAF, PANEL), BF16),
             V((2, 8, 128), F32),
             V((2, NCOL, 8, 128), F32),
             V((1, 128), F32),
@@ -540,10 +580,10 @@
         copy_out,
         out_shape=shapes,
         in_specs=[vmem] * 2,
-        out_specs=(vmem, vmem),
-        compiler_params=pltpu.CompilerParams(vmem_limit_bytes=60 * 2**20),
+        out_specs=(anywhere, anywhere),
+        scratch_shapes=[DMA((2,))],
         name="results",
-    )(vectors, hessen)
+    )(pltpu.with_memory_space_constraint(vectors, V), pltpu.with_memory_space_constraint(hessen, V))
 
 
 def solution(mesh):

time: 44.7 us -> 43 us (0.962)
  Pallas kernels: 43.9 us -> 42.2 us
    pallas_call x1, Pallas kernels: 42.5 us -> 41.6 us  [shards(): pl.pallas_call(kernel, out_shape=(V((2, LEAF, PANEL), F32), V((2, KRY + 2...]
    pallas_call x1, Pallas kernels: 1.38 us -> 0.64 us  [shards(): pl.pallas_call(copy_out, out_shape=shapes, in_specs=[vmem] * 2, out_specs...]
where the time goes in v3:
time: 43 us; the launch traced here: 42.9 us
  Pallas kernels  42.2 us (98%)
  between operations  0.64 us (1%)
    pallas_call x1, Pallas kernels, shards(): pl.pallas_call(kernel, out_shape=(V((2, LEAF, PANEL), F32), V((2, KRY + 2...  41.6 us

profile of v3, /device:TPU:1, one launch (start us, length us, event | category | flops | bytes accessed | tf_op | source)
XLA Modules:
  0.0 42.9 jit_solution(17145345544278209265)
XLA Ops:
  0.6 41.6 %hmatrix_gmres.1 = (f32[2,16,256]{2,1,0:T(8,128)S(1)}, f32[2,10]{1,0:T(2,128)S(1)}) custom-call(f32[8,16,256]{2,1,0:T(8,128)} %kry_h.1, f32[16,256]{1,0:T(8,128)} %sw_h.1, bf16[16,64,256]{2,1,0:T(8,128)(2,1)} %cb_h.1, f32[16,64,64]{2,1,0:T(8,128)} %tr_h.1, bf16[16,2,256,256]{3,2,1,0:T(8,128)(2,1)} %nb_h.1, f32[64,64,64]{2,1,0:T(8,128)} %bitcast.7, ...), custom_call_target="tpu_custom_call" | custom-call | tf_op jit(solution)/shard_map/hmatrix_gmres/pallas_call | solution.py:508
  42.2 0.6 %results.1 = (f32[2,16,256]{2,1,0:T(8,128)}, f32[2,10]{1,0:T(2,128)}) custom-call(f32[2,16,256]{2,1,0:T(8,128)S(1)} %get-tuple-element.4.v_in, f32[2,10]{1,0:T(2,128)S(1)} %get-tuple-element.5.h_in), custom_call_target="tpu_custom_call" | custom-call | tf_op jit(solution)/shard_map/results/pallas_call | solution.py:579

commit v4 on v3

--- a/solution.py
+++ b/solution.py
@@ -431,28 +431,27 @@
     near = near_new()
     wait(half, qf_r)
     gather_given()
+    wait(tab[1].at[pl.ds(0, NROW - 1)], pay_r.at[1])
+    tot = pltpu.roll(tree(tab[1][...])[2:3], 64, 1) * (1.0 / COUNT)
+    hs = [pick(tot, k) for k in range(KRY)]
+
+    def less(v, of):
+        for k in range(KRY):
+            v = v - hs[k] * of[k]
+        return v
+
+    send_near(1, less(near, nq))
+    far_part(1, *[less(g, qrows.at[:, p]) for p, g in enumerate(gather(1))])
     gsum = jnp.sum(qtab[:, :, QROWS - 1 : QROWS, :].reshape(NROW, 1, 128), axis=0) * (1.0 / COUNT)
     gram = jnp.zeros((8, 128), F32)
     for k in range(KRY):
         gram = jnp.where(iota((8, 128), 0) == k, pltpu.roll(gsum, 64 - 8 * k, 1), gram)
     gram = jnp.where(iota((8, 128), 1) < KRY, gram, 0.0)
-
-    wait(tab[1].at[pl.ds(0, NROW - 1)], pay_r.at[1])
-    tot = pltpu.roll(tree(tab[1][...])[2:3], 64, 1) * (1.0 / COUNT)
     h_row = jnp.where(lane1 < KRY, tot, 0.0)
     hh = jnp.sum(h_row * h_row, axis=1, keepdims=True)
     norm = pick(tot, KRY) - 2.0 * hh + quadratic(h_row)
     beta = jnp.sqrt(jnp.maximum(norm, 0.0) + 1e-06)
     inv = 1.0 / beta
-    hs = [pick(tot, k) for k in range(KRY)]
-
-    def less(v, of):
-        for k in range(KRY):
-            v = v - hs[k] * of[k]
-        return v
-
-    send_near(1, less(near, nq))
-    far_part(1, *[less(g, qrows.at[:, p]) for p, g in enumerate(gather(1))])
     q = less(w, kry) * inv
     out_v[0] = q
     line = jnp.where(lane1 == KRY + 1, beta, h_row)

time: 43 us -> 43 us (level)
  no operation moved by 1% of the time
where the time goes in v4:
time: 43 us; the launch traced here: 42.9 us
  Pallas kernels  42.2 us (98%)
  between operations  0.64 us (1%)
    pallas_call x1, Pallas kernels, shards(): pl.pallas_call(kernel, out_shape=(V((2, LEAF, PANEL), F32), V((2, KRY + 2...  41.6 us

profile of v4, /device:TPU:1, one launch (start us, length us, event | category | flops | bytes accessed | tf_op | source)
XLA Modules:
  0.0 42.9 jit_solution(13131956482284840693)
XLA Ops:
  0.6 41.6 %hmatrix_gmres.1 = (f32[2,16,256]{2,1,0:T(8,128)S(1)}, f32[2,10]{1,0:T(2,128)S(1)}) custom-call(f32[8,16,256]{2,1,0:T(8,128)} %kry_h.1, f32[16,256]{1,0:T(8,128)} %sw_h.1, bf16[16,64,256]{2,1,0:T(8,128)(2,1)} %cb_h.1, f32[16,64,64]{2,1,0:T(8,128)} %tr_h.1, bf16[16,2,256,256]{3,2,1,0:T(8,128)(2,1)} %nb_h.1, f32[64,64,64]{2,1,0:T(8,128)} %bitcast.7, ...), custom_call_target="tpu_custom_call" | custom-call | tf_op jit(solution)/shard_map/hmatrix_gmres/pallas_call | solution.py:507
  42.2 0.6 %results.1 = (f32[2,16,256]{2,1,0:T(8,128)}, f32[2,10]{1,0:T(2,128)}) custom-call(f32[2,16,256]{2,1,0:T(8,128)S(1)} %get-tuple-element.4.v_in, f32[2,10]{1,0:T(2,128)S(1)} %get-tuple-element.5.h_in), custom_call_target="tpu_custom_call" | custom-call | tf_op jit(solution)/shard_map/results/pallas_call | solution.py:578

commit v5 on v3

--- a/solution.py
+++ b/solution.py
@@ -196,9 +196,6 @@
 
     to_neighbours(halo_src, halo.at[0], halo.at[1], halo_s.at[0], halo_r.at[0])
     send_pay(0)
-
-    own = vq.at[pl.ds(LEAF, LEAF)]
-    to_neighbours(own, vq.at[pl.ds(0, LEAF)], vq.at[pl.ds(2 * LEAF, LEAF)], vq_s, vq_r)
 
     for k in range(KRY):
         for l in range(k, KRY):
@@ -404,6 +401,9 @@
         wait(halo.at[j], halo_r.at[0, j])
         vpad[0][2 * LEAF * j : 2 * LEAF * j + LEAF, :] = halo[j].astype(F32)
     send_near(0, near_last())
+    own = vq.at[pl.ds(LEAF, LEAF)]
+    to_neighbours(own, vq.at[pl.ds(0, LEAF)], vq.at[pl.ds(2 * LEAF, LEAF)], vq_s, vq_r)
+
     wait(tab[0].at[pl.ds(0, NROW - 1)], pay_r.at[0])
     far_part(0, *gather(0))
     l_sw.wait()

time: 43 us -> 43 us (level)
  no operation moved by 1% of the time
where the time goes in v5:
time: 43 us; the launch traced here: 42.9 us
  Pallas kernels  42.3 us (98%)
  between operations  0.64 us (1%)
    pallas_call x1, Pallas kernels, shards(): pl.pallas_call(kernel, out_shape=(V((2, LEAF, PANEL), F32), V((2, KRY + 2...  41.6 us

profile of v5, /device:TPU:1, one launch (start us, length us, event | category | flops | bytes accessed | tf_op | source)
XLA Modules:
  0.0 42.9 jit_solution(17342758493053044573)
XLA Ops:
  0.6 41.6 %hmatrix_gmres.1 = (f32[2,16,256]{2,1,0:T(8,128)S(1)}, f32[2,10]{1,0:T(2,128)S(1)}) custom-call(f32[8,16,256]{2,1,0:T(8,128)} %kry_h.1, f32[16,256]{1,0:T(8,128)} %sw_h.1, bf16[16,64,256]{2,1,0:T(8,128)(2,1)} %cb_h.1, f32[16,64,64]{2,1,0:T(8,128)} %tr_h.1, bf16[16,2,256,256]{3,2,1,0:T(8,128)(2,1)} %nb_h.1, f32[64,64,64]{2,1,0:T(8,128)} %bitcast.7, ...), custom_call_target="tpu_custom_call" | custom-call | tf_op jit(solution)/shard_map/hmatrix_gmres/pallas_call | solution.py:508
  42.3 0.6 %results.1 = (f32[2,16,256]{2,1,0:T(8,128)}, f32[2,10]{1,0:T(2,128)}) custom-call(f32[2,16,256]{2,1,0:T(8,128)S(1)} %get-tuple-element.4.v_in, f32[2,10]{1,0:T(2,128)S(1)} %get-tuple-element.5.h_in), custom_call_target="tpu_custom_call" | custom-call | tf_op jit(solution)/shard_map/results/pallas_call | solution.py:579
